TPU v7x, 128 devices: a whole 4x4x4 slice. The times are simulated.
128 devices in a mesh: row: 16 (over x, y), col: 8 (over z, core).
Axes of the slice: x: 4, y: 4, z: 4, core: 2. Of those that a mesh axis runs over, the one named last changes fastest.
Arguments:
- eigenvectors: float32 [98304, 2048], P('row', 'col'), may hold values from -6 to 6
- reflectors: float32 [98304, 512], P('row', 'col'), may hold values from -0.01953125 to 0.01953125
- triangles: float32 [16, 32, 32], replicated, as said below
Outputs:
- transformed: float32 [98304, 2048], P('row', 'col')
Inputs may be any that keep to these rules, and one draw needn't show every extreme that they name: Each triangles[k] is upper triangular with diagonal entries between 1.5 and 2.
All inputs are finite; a program needn't handle non-finite values.
Results may differ from a plain program's by a relative error of at most 0.0001.
Values sent between devices are 32-bit elements; how exact they have to be, the bound alone decides.
A program may use at most 128 MiB of HBM per device.

v0:
```python
import jax
import jax.numpy as jnp
from jax import lax
from jax.sharding import PartitionSpec as P


def on_device(eigenvectors, reflectors, triangles):
    highest = lax.Precision.HIGHEST
    everyone = lax.all_gather(reflectors, "col", axis=1, tiled=True)
    panel_count = triangles.shape[0]
    panel_width = triangles.shape[1]
    steps_total, step_width, factors = (panel_count, panel_width, triangles)

    def apply_panel(step_no, current):
        which_one = steps_total - 1 - step_no
        vectors = lax.dynamic_slice_in_dim(everyone, which_one * step_width, step_width, 1)
        partial_rows = jnp.einsum("rk,rc->kc", vectors, current, precision=highest)
        summed = lax.psum(partial_rows, "row")
        factor_now = lax.dynamic_index_in_dim(factors, which_one, 0, keepdims=False)
        scaled = jnp.dot(factor_now, summed, precision=highest)
        return current - jnp.dot(vectors, scaled, precision=highest)

    return lax.fori_loop(0, steps_total, apply_panel, eigenvectors)


def solution(mesh):
    return jax.shard_map(
        on_device,
        mesh=mesh,
        in_specs=(P("row", "col"), P("row", "col"), P()),
        out_specs=P("row", "col"),
        check_vma=False,
    )
```

profile of v0, /device:TPU:0, one launch (start us, length us, event | category | flops | bytes accessed | tf_op | source)
XLA Modules:
  0.0 1464.2 jit_solution(11301465494089690131)
XLA Ops:
  12.5 70.2 %all-gather.2.cloned.1.call-done = f32[6144,512]{0,1:T(8,128)} async-done(((f32[6144,64]{0,1:T(8,128)}), f32[6144,512]{0,1:T(8,128)}) %all-gather.2.cloned.1.call-update) | async-done | bytes 12582928 | tf_op jit(solution)/shard_map/all_gather | solution.py:9
  82.6 1374.7 %while.15 = (s32[]{:T(128)}, f32[6144,256]{1,0:T(8,128)}, f32[6144,512]{0,1:T(8,128)}, f32[16,32,32]{2,1,0:T(8,128)}, s32[]{:T(128)}, /*index=5*/s32[]{:T(128)}, s32[]{:T(128)}, s32[]{:T(128)}, s32[]{:T(128)}, s32[]{:T(128)}) while((s32[]{:T(128)}, f32[6144,256]{1,0:T(8,128)}, f32[6144,512]{0,1:T(8,128)}, f32[16,32,32]{2,1,0:T(8,128)}, ...), condition=%wide.region_2.3_spmd, body=%wide.region_0.2_spmd.sunk | while | flops 1212686336 | bytes 20660436 | solution.py:23
  88.8 74.3 %psum.15 = f32[32,256]{1,0:T(8,128)S(1)} all-reduce(f32[32,256]{1,0:T(8,128)S(1)} %fusion.26), channel_id=1, replica_groups=mesh['row'=16,'col'=8] {'row'}, use_global_device_ids=true, to_apply=%region_1.0 | all-reduce | flops 8192 | bytes 65536 | tf_op jit(solution)/shard_map/while/body/eval_jaxpr/psum | solution.py:18
  164.0 9.0 convolution_subtract_fusion.2
  179.2 69.5 %psum.15 = f32[32,256]{1,0:T(8,128)S(1)} all-reduce(f32[32,256]{1,0:T(8,128)S(1)} %fusion.26), channel_id=1, replica_groups=mesh['row'=16,'col'=8] {'row'}, use_global_device_ids=true, to_apply=%region_1.0 | all-reduce | flops 8192 | bytes 65536 | tf_op jit(solution)/shard_map/while/body/eval_jaxpr/psum | solution.py:18
  249.6 9.0 convolution_subtract_fusion.2
  258.6 6.2 fusion.26
  264.8 69.5 %psum.15 = f32[32,256]{1,0:T(8,128)S(1)} all-reduce(f32[32,256]{1,0:T(8,128)S(1)} %fusion.26), channel_id=1, replica_groups=mesh['row'=16,'col'=8] {'row'}, use_global_device_ids=true, to_apply=%region_1.0 | all-reduce | flops 8192 | bytes 65536 | tf_op jit(solution)/shard_map/while/body/eval_jaxpr/psum | solution.py:18
  335.2 9.0 convolution_subtract_fusion.2
  344.2 6.2 fusion.26
  350.4 69.5 %psum.15 = f32[32,256]{1,0:T(8,128)S(1)} all-reduce(f32[32,256]{1,0:T(8,128)S(1)} %fusion.26), channel_id=1, replica_groups=mesh['row'=16,'col'=8] {'row'}, use_global_device_ids=true, to_apply=%region_1.0 | all-reduce | flops 8192 | bytes 65536 | tf_op jit(solution)/shard_map/while/body/eval_jaxpr/psum | solution.py:18
  420.8 9.0 convolution_subtract_fusion.2
  429.9 6.2 fusion.26
  436.0 69.5 %psum.15 = f32[32,256]{1,0:T(8,128)S(1)} all-reduce(f32[32,256]{1,0:T(8,128)S(1)} %fusion.26), channel_id=1, replica_groups=mesh['row'=16,'col'=8] {'row'}, use_global_device_ids=true, to_apply=%region_1.0 | all-reduce | flops 8192 | bytes 65536 | tf_op jit(solution)/shard_map/while/body/eval_jaxpr/psum | solution.py:18
  506.5 9.0 convolution_subtract_fusion.2
  515.5 6.2 fusion.26
  521.7 69.5 %psum.15 = f32[32,256]{1,0:T(8,128)S(1)} all-reduce(f32[32,256]{1,0:T(8,128)S(1)} %fusion.26), channel_id=1, replica_groups=mesh['row'=16,'col'=8] {'row'}, use_global_device_ids=true, to_apply=%region_1.0 | all-reduce | flops 8192 | bytes 65536 | tf_op jit(solution)/shard_map/while/body/eval_jaxpr/psum | solution.py:18
  592.1 9.0 convolution_subtract_fusion.2
  601.1 6.2 fusion.26
  607.3 69.5 %psum.15 = f32[32,256]{1,0:T(8,128)S(1)} all-reduce(f32[32,256]{1,0:T(8,128)S(1)} %fusion.26), channel_id=1, replica_groups=mesh['row'=16,'col'=8] {'row'}, use_global_device_ids=true, to_apply=%region_1.0 | all-reduce | flops 8192 | bytes 65536 | tf_op jit(solution)/shard_map/while/body/eval_jaxpr/psum | solution.py:18
  677.7 9.0 convolution_subtract_fusion.2
  686.7 6.2 fusion.26
  692.9 69.5 %psum.15 = f32[32,256]{1,0:T(8,128)S(1)} all-reduce(f32[32,256]{1,0:T(8,128)S(1)} %fusion.26), channel_id=1, replica_groups=mesh['row'=16,'col'=8] {'row'}, use_global_device_ids=true, to_apply=%region_1.0 | all-reduce | flops 8192 | bytes 65536 | tf_op jit(solution)/shard_map/while/body/eval_jaxpr/psum | solution.py:18
  763.3 9.0 convolution_subtract_fusion.2
  772.4 6.2 fusion.26
  778.5 69.5 %psum.15 = f32[32,256]{1,0:T(8,128)S(1)} all-reduce(f32[32,256]{1,0:T(8,128)S(1)} %fusion.26), channel_id=1, replica_groups=mesh['row'=16,'col'=8] {'row'}, use_global_device_ids=true, to_apply=%region_1.0 | all-reduce | flops 8192 | bytes 65536 | tf_op jit(solution)/shard_map/while/body/eval_jaxpr/psum | solution.py:18
  849.0 9.0 convolution_subtract_fusion.2
  858.0 6.2 fusion.26
  864.2 69.5 %psum.15 = f32[32,256]{1,0:T(8,128)S(1)} all-reduce(f32[32,256]{1,0:T(8,128)S(1)} %fusion.26), channel_id=1, replica_groups=mesh['row'=16,'col'=8] {'row'}, use_global_device_ids=true, to_apply=%region_1.0 | all-reduce | flops 8192 | bytes 65536 | tf_op jit(solution)/shard_map/while/body/eval_jaxpr/psum | solution.py:18
  934.6 9.0 convolution_subtract_fusion.2
  943.6 6.2 fusion.26
  949.8 69.5 %psum.15 = f32[32,256]{1,0:T(8,128)S(1)} all-reduce(f32[32,256]{1,0:T(8,128)S(1)} %fusion.26), channel_id=1, replica_groups=mesh['row'=16,'col'=8] {'row'}, use_global_device_ids=true, to_apply=%region_1.0 | all-reduce | flops 8192 | bytes 65536 | tf_op jit(solution)/shard_map/while/body/eval_jaxpr/psum | solution.py:18
  1020.2 9.0 convolution_subtract_fusion.2
  1029.2 6.2 fusion.26
  1035.4 69.5 %psum.15 = f32[32,256]{1,0:T(8,128)S(1)} all-reduce(f32[32,256]{1,0:T(8,128)S(1)} %fusion.26), channel_id=1, replica_groups=mesh['row'=16,'col'=8] {'row'}, use_global_device_ids=true, to_apply=%region_1.0 | all-reduce | flops 8192 | bytes 65536 | tf_op jit(solution)/shard_map/while/body/eval_jaxpr/psum | solution.py:18
  1105.8 9.0 convolution_subtract_fusion.2
  1114.9 6.2 fusion.26
  1121.0 69.5 %psum.15 = f32[32,256]{1,0:T(8,128)S(1)} all-reduce(f32[32,256]{1,0:T(8,128)S(1)} %fusion.26), channel_id=1, replica_groups=mesh['row'=16,'col'=8] {'row'}, use_global_device_ids=true, to_apply=%region_1.0 | all-reduce | flops 8192 | bytes 65536 | tf_op jit(solution)/shard_map/while/body/eval_jaxpr/psum | solution.py:18
  1191.5 9.0 convolution_subtract_fusion.2
  1200.5 6.2 fusion.26
  1206.7 69.5 %psum.15 = f32[32,256]{1,0:T(8,128)S(1)} all-reduce(f32[32,256]{1,0:T(8,128)S(1)} %fusion.26), channel_id=1, replica_groups=mesh['row'=16,'col'=8] {'row'}, use_global_device_ids=true, to_apply=%region_1.0 | all-reduce | flops 8192 | bytes 65536 | tf_op jit(solution)/shard_map/while/body/eval_jaxpr/psum | solution.py:18
  1277.1 9.0 convolution_subtract_fusion.2
  1286.1 6.2 fusion.26
  1292.3 69.5 %psum.15 = f32[32,256]{1,0:T(8,128)S(1)} all-reduce(f32[32,256]{1,0:T(8,128)S(1)} %fusion.26), channel_id=1, replica_groups=mesh['row'=16,'col'=8] {'row'}, use_global_device_ids=true, to_apply=%region_1.0 | all-reduce | flops 8192 | bytes 65536 | tf_op jit(solution)/shard_map/while/body/eval_jaxpr/psum | solution.py:18
  1362.7 9.0 convolution_subtract_fusion.2
  1371.7 6.2 fusion.26
  1377.9 69.5 %psum.15 = f32[32,256]{1,0:T(8,128)S(1)} all-reduce(f32[32,256]{1,0:T(8,128)S(1)} %fusion.26), channel_id=1, replica_groups=mesh['row'=16,'col'=8] {'row'}, use_global_device_ids=true, to_apply=%region_1.0 | all-reduce | flops 8192 | bytes 65536 | tf_op jit(solution)/shard_map/while/body/eval_jaxpr/psum | solution.py:18
  1448.3 9.0 convolution_subtract_fusion.2
  (21 shorter events, 32.2 us)
Async XLA Ops:
  6.5 76.1 %all-gather.2.cloned.1.call-start = ((), (), s32[]{:S(2)}) async-start(), calls=%async_computation | async-start | bytes 14155776 | tf_op jit(solution)/shard_map/all_gather | solution.py:9
Sparse Core Ops, SparseCore 0:
  12.6 70.0 all-gather.1
where the time goes:
time: 1470 us; the launch traced here: 1460 us
  blocking collectives  1120 us (76%)
  matrix products  257 us (17%)
  waiting for transfers between devices  70.2 us (5%)
    psum x16, blocking collectives, apply_panel(): summed = lax.psum(partial_rows, 'row')  1120 us
    dot_general x16, matrix products, apply_panel(): return current - jnp.dot(vectors, scaled, precision=highest)  145 us
    dot_general x16, matrix products, apply_panel(): partial_rows = jnp.einsum('rk,rc->kc', vectors, current, precision=highest)  98.6 us
    all_gather x1, waiting for transfers between devices, on_device(): everyone = lax.all_gather(reflectors, 'col', axis=1, tiled=True)  70.2 us
  transfers between devices with their start and end apart: 1, of which 1 were waited for; matrix products, arithmetic and copies ran while one was open for 0% of the time, Pallas kernels for 0%

commit v1 on v0

v1 whole, which is shorter than its diff:
```python
import jax
import jax.numpy as jnp
from jax import lax
from jax.sharding import PartitionSpec as P

HIGH = lax.Precision.HIGH
HIGHEST = lax.Precision.HIGHEST


def on_device(eigenvectors, reflectors, triangles):
    panels, width = triangles.shape[0], triangles.shape[1]
    everyone = lax.all_gather(reflectors, "col", axis=1, tiled=True)
    products = jnp.einsum("rk,rc->kc", everyone, eigenvectors, precision=HIGH)
    gram = jnp.einsum("rk,rc->kc", reflectors, everyone, precision=HIGH)
    products, gram = lax.psum((products, gram), "row")
    gram = lax.all_gather(gram, "col", axis=0, tiled=True)
    scaled = [None] * panels
    rest = products
    for k in range(panels - 1, -1, -1):
        now = jnp.dot(triangles[k], rest[k * width:], precision=HIGHEST)
        scaled[k] = now
        if k:
            rest = rest[:k * width] - jnp.dot(
                gram[:k * width, k * width:(k + 1) * width], now, precision=HIGHEST)
    return eigenvectors - jnp.dot(everyone, jnp.concatenate(scaled, 0), precision=HIGH)


def solution(mesh):
    return jax.shard_map(
        on_device,
        mesh=mesh,
        in_specs=(P("row", "col"), P("row", "col"), P()),
        out_specs=P("row", "col"),
        check_vma=False,
    )
```

time: 1470 us -> 255 us (0.17)
  blocking collectives: 1120 us -> 0 us
  matrix products: 257 us -> 50.8 us
  waiting for transfers between devices: 70.2 us -> 176 us
    psum x16 -> x0, blocking collectives: 1120 us -> none  [apply_panel(): summed = lax.psum(partial_rows, 'row')]
    dot_general x48 -> x34, matrix products: 257 us -> 50.8 us  [the longest x1 15.5 us: on_device(): jnp.dot(everyone, jnp.concatenate(scaled, 0), precision=HIGH)]
    psum x0 -> x1, waiting for transfers between devices: none -> 85.4 us  [on_device(): products, gram = lax.psum((products, gram), 'row')]
    all_gather x0 -> x1, waiting for transfers between devices: none -> 17.8 us  [on_device(): gram = lax.all_gather(gram, 'col', axis=0, tiled=True)]
  transfers between devices with their start and end apart: 1 -> 3, of which waited for: 1 -> 3; matrix products, arithmetic and copies ran while one was open for 0% -> 3% of each run, Pallas kernels for 0% -> 0%
where the time goes in v1:
time: 255 us; the launch traced here: 254 us
  waiting for transfers between devices  176 us (69%)
  matrix products  50.8 us (20%)
  between operations  13.5 us (5%)
  local copies, waits for them, and re-layouts  13.3 us (5%)
    psum x1, waiting for transfers between devices, on_device(): products, gram = lax.psum((products, gram), 'row')  85.4 us
    all_gather x1, waiting for transfers between devices, on_device(): everyone = lax.all_gather(reflectors, 'col', axis=1, tiled=True)  71.8 us
    all_gather x1, waiting for transfers between devices, on_device(): gram = lax.all_gather(gram, 'col', axis=0, tiled=True)  17.8 us
    dot_general x1, matrix products, on_device(): jnp.dot(everyone, jnp.concatenate(scaled, 0), precision=HIGH)  15.5 us
    dot_general x15, matrix products, on_device(): jnp.dot(gram[:k * width, k * width:(k + 1) * width], now, precision=HIGHEST)  13 us
    dot_general x1, matrix products, on_device(): gram = jnp.einsum('rk,rc->kc', reflectors, everyone, precision=HIGH)  11.7 us
    dot_general x1, matrix products, on_device(): products = jnp.einsum('rk,rc->kc', everyone, eigenvectors, precision=HIGH)  8.14 us
    unnamed x25, local copies, waits for them, and re-layouts  6.73 us
  transfers between devices with their start and end apart: 3, of which 3 were waited for; matrix products, arithmetic and copies ran while one was open for 3% of the time, Pallas kernels for 0%

profile of v1, /device:TPU:0, one launch (start us, length us, event | category | flops | bytes accessed | tf_op | source)
XLA Modules:
  0.0 253.6 jit_solution(4089848123566574349)
XLA Ops:
  6.5 0.0 all-gather.3.cloned.1.call-start
  6.5 0.7 all-gather.3.cloned.1.call-update
  7.3 0.0 all-reduce.3.cloned.1.call-start
  7.3 71.8 %all-gather.3.cloned.1.call-done = f32[6144,512]{0,1:T(8,128)} async-done(((f32[6144,64]{0,1:T(8,128)}), f32[6144,512]{0,1:T(8,128)}) %all-gather.3.cloned.1.call-update) | async-done | bytes 12582928 | tf_op jit(solution)/shard_map/all_gather | solution.py:12
  79.1 11.7 %fusion.80 = f32[64,512]{1,0:T(8,128)} fusion(f32[6144,64]{0,1:T(8,128)} %param.4, f32[6144,512]{0,1:T(8,128)} %all-gather.3.cloned.1.call-done), kind=kOutput, calls=%fused_computation.112 | convolution fusion | flops 1207959552 | bytes 14286848 | tf_op jit(solution)/shard_map/rk,rc->kc/dot_general | solution.py:14
  90.8 0.0 copy-done
  90.8 8.1 %fusion.79 = f32[512,256]{1,0:T(8,128)} fusion(f32[6144,512]{0,1:T(8,128)S(1)} %copy-done, f32[6144,256]{1,0:T(8,128)} %param.3), kind=kOutput, calls=%fused_computation.111 | convolution fusion | flops 4831838208 | bytes 19398656 | tf_op jit(solution)/shard_map/rk,rc->kc/dot_general | solution.py:13
  98.9 0.0 all-reduce.3.cloned.1.call-update
  98.9 0.2 all-gather.5.cloned.1.call-start
  99.2 85.4 %all-reduce.3.cloned.1.call-done = (f32[512,256]{1,0:T(8,128)}, f32[64,512]{1,0:T(8,128)}) async-done(((f32[512,256]{1,0:T(8,128)}, f32[64,512]{1,0:T(8,128)}), (f32[512,256]{1,0:T(8,128)}, f32[64,512]{1,0:T(8,128)})) %all-reduce.3.cloned.1.call-update) | async-done | bytes 655376 | tf_op jit(solution)/shard_map/psum | solution.py:15
  184.6 0.0 all-gather.5.cloned.1.call-update
  184.6 0.0 copy-start.4
  184.6 6.6 %copy.4 = f32[6144,256]{0,1:T(8,128)} copy(f32[6144,256]{1,0:T(8,128)} %param.3) | data formatting | bytes 12582912 | tf_op args[0]
  191.3 0.0 copy-done.3
  191.3 0.2 fusion.44
  191.4 17.8 %all-gather.5.cloned.1.call-done = f32[512,512]{1,0:T(8,128)} async-done(((f32[64,512]{1,0:T(8,128)}), f32[512,512]{1,0:T(8,128)}) %all-gather.5.cloned.1.call-update) | async-done | bytes 1048592 | tf_op jit(solution)/shard_map/all_gather | solution.py:16
  209.2 1.7 convolution_subtract_fusion
  211.0 0.2 fusion.42
  211.1 1.8 convolution_subtract_fusion.1
  213.0 0.2 fusion.40
  213.1 1.5 convolution_subtract_fusion.2
  214.6 0.2 fusion.38
  214.8 1.4 convolution_subtract_fusion.3
  216.2 0.2 fusion.36
  216.3 1.4 convolution_subtract_fusion.4
  217.8 0.2 fusion.34
  217.9 1.4 convolution_subtract_fusion.5
  219.3 0.2 fusion.32
  219.5 1.3 convolution_subtract_fusion.6
  220.8 0.2 fusion.30
  221.0 0.3 convolution_subtract_fusion.7
  221.4 0.2 fusion.28
  221.5 0.4 convolution_subtract_fusion.8
  221.9 0.2 fusion.26
  222.1 0.4 convolution_subtract_fusion.9
  222.5 0.2 fusion.24
  222.6 0.3 convolution_subtract_fusion.10
  223.0 0.2 fusion.22
  223.1 0.2 convolution_subtract_fusion.11
  223.4 0.2 fusion.20
  223.6 0.3 convolution_subtract_fusion.12
  223.9 0.2 fusion.17
  224.0 0.3 convolution_subtract_fusion.13
  224.3 0.2 fusion.15
  224.5 0.2 convolution_subtract_fusion.14
  224.7 0.2 fusion.1
  225.1 15.5 %fusion = f32[6144,256]{0,1:T(8,128)} fusion(f32[6144,256]{0,1:T(8,128)S(1)} %copy-done.1, f32[512,256]{1,0:T(8,128)S(1)} %constant_dynamic-update-slice_fusion, f32[6144,512]{0,1:T(8,128)} %all-gather.3.cloned.1.call-done), kind=kOutput, calls=%fused_computation.1 | convolution fusion | flops 4833411072 | bytes 25690112 | tf_op jit(solution)/shard_map/dot_general | solution.py:25
  240.5 6.6 %copy.5 = f32[6144,256]{1,0:T(8,128)} copy(f32[6144,256]{0,1:T(8,128)} %fusion) | data formatting | bytes 12582912 | tf_op jit(solution)/shard_map/sub | solution.py:25
  (22 shorter events, 0.1 us)
Async XLA Ops:
  6.5 72.6 %all-gather.3.cloned.1.call-start = ((), (), s32[]{:S(2)}) async-start(), calls=%async_computation | async-start | bytes 14155776 | tf_op jit(solution)/shard_map/all_gather | solution.py:12
  7.3 177.3 %all-reduce.3.cloned.1.call-start = ((), (), s32[]{:S(2)}) async-start(), calls=%async_computation.2 | async-start | bytes 1310720 | tf_op jit(solution)/shard_map/psum | solution.py:15
  79.1 11.7 %copy-start = (f32[6144,512]{0,1:T(8,128)S(1)}, f32[6144,512]{0,1:T(8,128)}, u32[]{:S(2)}) copy-start(f32[6144,512]{0,1:T(8,128)} %all-gather.3.cloned.1.call-done) | copy-start | bytes 37748740
  98.9 110.3 %all-gather.5.cloned.1.call-start = ((), (), s32[]{:S(2)}) async-start(), calls=%async_computation.1 | async-start | bytes 1179648 | tf_op jit(solution)/shard_map/all_gather | solution.py:16
  184.6 6.7 %copy-start.3 = (f32[512,256]{1,0:T(8,128)S(1)}, f32[512,256]{1,0:T(8,128)}, u32[]{:S(2)}) copy-start(f32[512,256]{1,0:T(8,128)} %get-tuple-element.5) | copy-start | bytes 1572868
  184.6 6.7 %copy-start.4 = (f32[16,32,32]{2,1,0:T(8,128)S(1)}, f32[16,32,32]{2,1,0:T(8,128)}, u32[]{:S(2)}) copy-start(f32[16,32,32]{2,1,0:T(8,128)} %param.5) | copy-start | bytes 196612
  209.2 11.8 %copy-start.2 = (f32[512,512]{1,0:T(8,128)S(1)}, f32[512,512]{1,0:T(8,128)}, u32[]{:S(2)}) copy-start(f32[512,512]{1,0:T(8,128)} %all-gather.5.cloned.1.call-done) | copy-start | bytes 3145732
  209.2 15.8 %copy-start.1 = (f32[6144,256]{0,1:T(8,128)S(1)}, f32[6144,256]{0,1:T(8,128)}, u32[]{:S(2)}) copy-start(f32[6144,256]{0,1:T(8,128)} %copy.4) | copy-start | bytes 18874372
Sparse Core Ops, SparseCore 0:
  9.0 70.0 all-gather.2
  99.1 85.4 all-reduce.2
  186.3 22.8 all-gather.4

commit v2 on v0

v2 whole, which is shorter than its diff:
```python
import functools

import jax
import jax.numpy as jnp
from jax import lax
from jax.experimental import pallas as pl
from jax.experimental.pallas import tpu as pltpu
from jax.sharding import PartitionSpec as P

MESH = pl.DeviceIdType.MESH
HIGHEST = lax.Precision.HIGHEST
F32, BF16 = jnp.float32, jnp.bfloat16
CHUNKS = 8
OWN, UP, DOWN, FAR = range(4)
REL = (0, 1, 3, 2)
GRAM = ((OWN, UP), (UP, UP), (OWN, DOWN), (UP, DOWN), (OWN, OWN), (DOWN, DOWN),
        (UP, FAR), (FAR, FAR), (DOWN, FAR), (OWN, FAR))


def split(a):
    high = a.astype(BF16)
    return high, (a - high.astype(F32)).astype(BF16)


def dot3(a, b, dims=(((1,), (0,)), ((), ()))):
    d = functools.partial(lax.dot_general, dimension_numbers=dims, preferred_element_type=F32)
    return d(a[0], b[0]) + (d(a[0], b[1]) + d(a[1], b[0]))


NT = (((1,), (1,)), ((), ()))


def gather_kernel(rows, vt_in, x_in, t_ref, wh_ref, wl_ref, vnh_out, vnl_out,
                  vt, xb, xh, xl, vnh, vnl, pacc, pred, gacc, gh, gf, mref,
                  rs_e, rs_g, rs_l,
                  lsem, xsem, sbs, sbr, zs, zr, rss, rsr, ags, agr, gxs, gxr, osem):
    me = lax.axis_index("row")
    col = lax.axis_index("col")
    z, k = lax.div(col, 2), lax.rem(col, 2)
    up = lax.rem(z + 1, 4) * 2 + k
    down = lax.rem(z + 3, 4) * 2 + k
    sib = z * 2 + 1 - k
    lanes = vt.shape[-1]

    barrier = pltpu.get_barrier_semaphore()
    for other in (up, down, sib):
        pl.semaphore_signal(barrier, inc=1, device_id=(me, other), device_id_type=MESH)
    for d in range(1, rows):
        pl.semaphore_signal(barrier, inc=1, device_id=(lax.rem(me + d, rows), col), device_id_type=MESH)

    def own(c):
        return vt_in.at[:, pl.ds(pl.multiple_of(c * lanes, lanes), lanes)]

    def local(c):
        return pltpu.make_async_copy(own(c), vt.at[OWN, c, k], lsem.at[c])

    def load_x(c):
        return pltpu.make_async_copy(x_in.at[pl.ds(pl.multiple_of(c * lanes, lanes), lanes)], xb.at[c], xsem.at[c])

    def remote(src, dst, ssem, rsem, target):
        return pltpu.make_async_remote_copy(src_ref=src, dst_ref=dst, send_sem=ssem, recv_sem=rsem,
                                            device_id=target, device_id_type=MESH)

    def z_own(way, c):
        return remote(own(c), vt.at[(UP, DOWN)[way], c, k], zs.at[way, c], zr.at[way, c], (me, (down, up)[way]))

    def z_pass(way, j):
        c = (j, CHUNKS // 2 + j)[way]
        return remote(vt.at[(UP, DOWN)[way], c, k], vt.at[FAR, c, k],
                      zs.at[way, CHUNKS + j], zr.at[way, CHUNKS + j], (me, (down, up)[way]))

    def to_sib(slot, c):
        src = own(c) if slot == OWN else vt.at[slot, c, k]
        return remote(src, vt.at[slot, c, k], sbs.at[slot, c], sbr.at[slot, c], (me, sib))

    def peer(d):
        return lax.rem(me + d, rows)

    def rs(kind, d):
        p = peer(d)
        src = (pacc.at[pl.ds(0, 3), p], gacc.at[pl.ds(3 * p, 3)], pacc.at[pl.ds(3, 1), p])[kind]
        dst = (rs_e, rs_g, rs_l)[kind].at[d]
        return remote(src, dst, rss.at[kind, d], rsr.at[kind, d], (p, col))

    def piece(kind, owner):
        return (pred.at[pl.ds(0, 3), owner], gh.at[k, pl.ds(3 * owner, 3)], pred.at[pl.ds(3, 1), owner])[kind]

    def ag_send(kind, d):
        return remote(piece(kind, me), piece(kind, me), ags.at[kind, d], agr.at[kind, d], (peer(d), col))

    def ag_recv(kind, d):
        source = lax.rem(me + rows - d, rows)
        return remote(piece(kind, source), piece(kind, source), ags.at[kind, d], agr.at[kind, d], (peer(d), col))

    def each(fn):
        lax.fori_loop(1, rows, lambda d, _: (fn(d), 0)[1], 0)

    def reduce_scatter(kind):
        each(lambda d: rs(kind, d).start())

    def sum_and_gather(kind):
        each(lambda d: rs(kind, d).wait_recv())
        buf = (rs_e, rs_g, rs_l)[kind]
        total = (pacc[0:3, me], gacc[pl.ds(3 * me, 3)], pacc[3:4, me])[kind]
        for d in range(1, rows):
            total = total + buf[d]
        if kind == 1:
            gh[k, pl.ds(3 * me, 3)] = total
        elif kind == 0:
            pred[0:3, me] = total
        else:
            pred[3:4, me] = total
        each(lambda d: ag_send(kind, d).start())

    def finish_gather(kind):
        each(lambda d: ag_recv(kind, d).wait_recv())

    def gx(i):
        half = pl.ds(0, 48)
        if i == 0:
            return remote(gh.at[k, pl.ds(0, 16)], gh.at[k, pl.ds(48, 16)], gxs.at[0], gxr.at[0], (me, down))
        if i == 1:
            return remote(gh.at[k, pl.ds(16, 16)], gh.at[k, pl.ds(64, 16)], gxs.at[1], gxr.at[1], (me, up))
        if i == 3:
            half = pl.ds(48, 32)
        return remote(gh.at[k, half], gh.at[k, half], gxs.at[i], gxr.at[i], (me, sib))

    def store_out(c):
        return (pltpu.make_async_copy(vnh.at[c], vnh_out.at[c], osem.at[0, c]),
                pltpu.make_async_copy(vnl.at[c], vnl_out.at[c], osem.at[1, c]))

    def block(slot, c):
        return vt[slot, c].reshape(2 * vt.shape[3], lanes)

    def apply(slot, c, first):
        v = block(slot, c)
        p = dot3(split(v), (xh[c], xl[c])).reshape(16, 8, 256)
        th, tl = split(v.T)
        vnh[c, :, slot * 128:(slot + 1) * 128] = th
        vnl[c, :, slot * 128:(slot + 1) * 128] = tl
        pacc[slot] += p

    def gram(c):
        v = [split(block(s, c)) for s in (OWN, UP, DOWN)]
        a = [split(vt[s, c, k]) for s in (OWN, UP, DOWN)]
        for i, (r, s) in enumerate(GRAM[:6]):
            gacc[8 * i:8 * i + 8] += dot3(a[r], v[s], NT).reshape(8, 8, 128)

    for c in range(CHUNKS):
        local(c).start()
        load_x(c).start()
    pl.semaphore_wait(barrier, rows + 2)
    for c in range(2):
        for way in range(2):
            z_own(way, c).start()
    for c in range(CHUNKS):
        to_sib(OWN, c).start()
    pacc[...] = jnp.zeros_like(pacc)
    gacc[...] = jnp.zeros_like(gacc)

    def neighbours(c):
        to_sib(UP, c).wait_recv()
        to_sib(DOWN, c).wait_recv()
        apply(UP, c, False)
        apply(DOWN, c, False)
        gram(c)

    def step(c, _):
        load_x(c).wait()
        h, l = split(xb[c])
        xh[c] = h
        xl[c] = l
        local(c).wait()
        to_sib(OWN, c).wait_recv()
        apply(OWN, c, False)

        @pl.when(c > 0)
        def _():
            neighbours(c - 1)

        z_own(0, c).wait_recv()
        z_own(1, c).wait_recv()

        @pl.when(c < CHUNKS - 2)
        def _():
            z_own(0, c + 2).start()
            z_own(1, c + 2).start()

        @pl.when(c >= CHUNKS - 2)
        def _():
            z_pass(0, c - (CHUNKS - 2)).start()
            z_pass(1, c - (CHUNKS - 2)).start()

        to_sib(UP, c).start()
        to_sib(DOWN, c).start()
        return 0

    lax.fori_loop(0, CHUNKS, step, 0)

    def far(j):
        def one(i, _):
            c = j + i * (CHUNKS // 2)
            to_sib(FAR, c).wait_recv()
            apply(FAR, c, True)
            a, b = store_out(c)
            a.start()
            b.start()
            return 0
        lax.fori_loop(0, 2, one, 0)

    def arrived(j):
        z_pass(0, j).wait_recv()
        z_pass(1, j).wait_recv()
        if j + 2 < CHUNKS // 2:
            z_pass(0, j + 2).start()
            z_pass(1, j + 2).start()
        to_sib(FAR, j).start()
        to_sib(FAR, CHUNKS // 2 + j).start()

    neighbours(CHUNKS - 1)
    reduce_scatter(1)
    reduce_scatter(0)
    arrived(0)
    sum_and_gather(1)
    far(0)
    sum_and_gather(0)
    finish_gather(1)
    gx(0).start()
    gx(1).start()
    gx(2).start()
    arrived(1)
    far(1)
    gx(0).wait_recv()
    gx(1).wait_recv()
    gx(3).start()
    arrived(2)
    far(2)
    gx(2).wait_recv()
    gx(3).wait_recv()
    for i, (r, s) in enumerate(GRAM):
        full = gh[:, 8 * i:8 * i + 8].reshape(128, 128)
        gf[r, s] = full
        if r != s:
            gf[s, r] = full.T
    mref[...] = jnp.zeros_like(mref)
    at_row = lax.broadcasted_iota(jnp.int32, (32, 128), 0)
    at_col = lax.broadcasted_iota(jnp.int32, (32, 128), 1)
    for i in range(3, -1, -1):
        part = slice(32 * i, 32 * i + 32)
        unit = jnp.where(at_col == at_row + 32 * i, 1.0, 0.0).astype(F32)
        for slot in range(4):
            shard = lax.rem(z + REL[slot], 4)
            rest = unit - jnp.dot(gf[slot, slot, part, :], mref[slot], precision=HIGHEST)
            mref[slot, part, :] = jnp.dot(t_ref[4 * shard + i], rest, precision=HIGHEST)
    finish_gather(0)

    arrived(3)
    far(3)
    reduce_scatter(2)
    sum_and_gather(2)
    finish_gather(2)

    def slot_of(shard):
        rel = lax.rem(shard - z + 4, 4)
        return rel + lax.div(rel, 2) - 2 * lax.div(rel, 3)

    slots = [slot_of(s) for s in range(4)]
    rest = [pred[slots[s]].reshape(128, 256) for s in range(4)]
    for s in range(3, -1, -1):
        w = jnp.dot(mref[slots[s]], rest[s], precision=HIGHEST)
        h, l = split(w)
        at = pl.ds(pl.multiple_of(slots[s] * 128, 128), 128)
        wh_ref[at] = h
        wl_ref[at] = l
        for r in range(s):
            rest[r] = rest[r] - jnp.dot(gf[slots[r], slots[s]], w, precision=HIGHEST)

    def sent(c, _):
        for way in range(2):
            z_own(way, c).wait_send()
        for slot in range(4):
            to_sib(slot, c).wait_send()
        for copy in store_out(c):
            copy.wait()
        return 0

    lax.fori_loop(0, CHUNKS, sent, 0)
    for j in range(CHUNKS // 2):
        z_pass(0, j).wait_send()
        z_pass(1, j).wait_send()
    for i in range(4):
        gx(i).wait_send()

    def sent_d(d):
        for kind in range(3):
            rs(kind, d).wait_send()
            ag_send(kind, d).wait_send()

    each(sent_d)


def update_kernel(x_ref, vh_ref, vl_ref, wh_ref, wl_ref, o_ref):
    o_ref[...] = x_ref[...] - dot3((vh_ref[0], vl_ref[0]), (wh_ref[...], wl_ref[...]))


def on_device(rows, eigenvectors, reflectors, triangles):
    height, width = eigenvectors.shape
    lanes = height // CHUNKS
    half = reflectors.shape[1]
    dma = pltpu.SemaphoreType.DMA
    anywhere = pl.BlockSpec(memory_space=pl.ANY)
    vmem = pl.BlockSpec(memory_space=pltpu.VMEM)
    wh, wl, vnh, vnl = pl.pallas_call(
        functools.partial(gather_kernel, rows),
        out_shape=[
            jax.ShapeDtypeStruct((512, width), BF16),
            jax.ShapeDtypeStruct((512, width), BF16),
            jax.ShapeDtypeStruct((CHUNKS, lanes, 512), BF16),
            jax.ShapeDtypeStruct((CHUNKS, lanes, 512), BF16),
        ],
        in_specs=[anywhere, anywhere, vmem],
        out_specs=[vmem, vmem, anywhere, anywhere],
        scratch_shapes=[
            pltpu.VMEM((4, CHUNKS, 2, half, lanes), F32),
            pltpu.VMEM((CHUNKS, lanes, width), F32),
            pltpu.VMEM((CHUNKS, lanes, width), BF16),
            pltpu.VMEM((CHUNKS, lanes, width), BF16),
            pltpu.VMEM((CHUNKS, lanes, 512), BF16),
            pltpu.VMEM((CHUNKS, lanes, 512), BF16),
            pltpu.VMEM((4, 16, 8, width), F32),
            pltpu.VMEM((4, 16, 8, width), F32),
            pltpu.VMEM((48, 8, 128), F32),
            pltpu.VMEM((2, 80, 8, 128), F32),
            pltpu.VMEM((4, 4, 128, 128), F32),
            pltpu.VMEM((4, 128, 128), F32),
            pltpu.VMEM((16, 3, 8, width), F32),
            pltpu.VMEM((16, 3, 8, 128), F32),
            pltpu.VMEM((16, 1, 8, width), F32),
            dma((CHUNKS,)), dma((CHUNKS,)),
            dma((4, CHUNKS)), dma((4, CHUNKS)),
            dma((2, CHUNKS + CHUNKS // 2)), dma((2, CHUNKS + CHUNKS // 2)),
            dma((3, 16)), dma((3, 16)), dma((3, 16)), dma((3, 16)),
            dma((4,)), dma((4,)), dma((2, CHUNKS)),
        ],
        compiler_params=pltpu.CompilerParams(
            collective_id=0, has_side_effects=True, vmem_limit_bytes=56 * 2**20),
    )(reflectors.T, eigenvectors, triangles)
    whole = pl.BlockSpec((512, width), lambda i: (0, 0))
    tall = pl.BlockSpec((1, lanes, 512), lambda i: (i, 0, 0))
    rowwise = pl.BlockSpec((lanes, width), lambda i: (i, 0))
    return pl.pallas_call(
        update_kernel,
        grid=(CHUNKS,),
        out_shape=jax.ShapeDtypeStruct((height, width), F32),
        in_specs=[rowwise, tall, tall, whole, whole],
        out_specs=rowwise,
        compiler_params=pltpu.CompilerParams(vmem_limit_bytes=32 * 2**20),
    )(eigenvectors, vnh, vnl, wh, wl)


def solution(mesh):
    return jax.shard_map(
        functools.partial(on_device, mesh.shape["row"]),
        mesh=mesh,
        in_specs=(P("row", "col"), P("row", "col"), P()),
        out_specs=P("row", "col"),
        check_vma=False,
    )
```

time: 1470 us -> 105 us (0.07)
  blocking collectives: 1120 us -> 0 us
  matrix products: 257 us -> 0 us
  Pallas kernels: 0 us -> 97.3 us
  waiting for transfers between devices: 70.2 us -> 0 us
    psum x16 -> x0, blocking collectives: 1120 us -> none  [apply_panel(): summed = lax.psum(partial_rows, 'row')]
    dot_general x48 -> x0, matrix products: 257 us -> none  [the longest x16 145 us: apply_panel(): return current - jnp.dot(vectors, scaled, precision=highest)]
    pallas_call x0 -> x2, Pallas kernels: none -> 97.3 us  [the longest x1 89.8 us: on_device(): pl.pallas_call(functools.partial(gather_kernel, rows), out_shape=[jax.Sha...]
    all_gather x1 -> x0, waiting for transfers between devices: 70.2 us -> none  [on_device(): everyone = lax.all_gather(reflectors, 'col', axis=1, tiled=True)]
  transfers between devices with their start and end apart: 1 -> 0, of which waited for: 1 -> 0; matrix products, arithmetic and copies ran while one was open for 0% -> 0% of each run, Pallas kernels for 0% -> 0%
where the time goes in v2:
time: 105 us
  Pallas kernels  97.3 us (93%)
  local copies, waits for them, and re-layouts  7.46 us (7%)
    pallas_call x1, Pallas kernels, on_device(): pl.pallas_call(functools.partial(gather_kernel, rows), out_shape=[jax.Sha...  89.8 us
    unnamed x10, local copies, waits for them, and re-layouts  7.46 us
    pallas_call x1, Pallas kernels, on_device(): pl.pallas_call(update_kernel, grid=(CHUNKS,), out_shape=jax.ShapeDtypeStr...  7.42 us

profile of v2, /device:TPU:0, one launch (start us, length us, event | category | flops | bytes accessed | tf_op | source)
XLA Modules:
  0.0 104.7 jit_solution(4941095699432997097)
XLA Ops:
  0.0 0.0 copy-start
  0.0 89.8 %shard_map.37 = (bf16[512,256]{1,0:T(8,128)(2,1)}, bf16[512,256]{1,0:T(8,128)(2,1)}, bf16[8,768,512]{2,1,0:T(8,128)(2,1)}, bf16[8,768,512]{2,1,0:T(8,128)(2,1)}) custom-call(f32[64,6144]{1,0:T(8,128)} %bitcast.1, f32[6144,256]{1,0:T(8,128)} %x_ref.1, f32[16,32,32]{2,1,0:T(8,128)} %t_ref.1), custom_call_target="tpu_custom_call" | custom-call | tf_op jit(solution)/shard_map/pallas_call | solution.py:313
  89.8 0.0 copy-done
  89.9 0.0 copy-start.1
  89.9 2.8 %copy-done.1 = bf16[8,768,512]{2,1,0:T(8,128)(2,1)S(1)} copy-done((bf16[8,768,512]{2,1,0:T(8,128)(2,1)S(1)}, bf16[8,768,512]{2,1,0:T(8,128)(2,1)}, u32[]{:S(2)}) %copy-start.1) | copy-done | bytes 6291480
  92.6 0.0 copy-start.2
  92.6 2.8 %copy-done.2 = bf16[8,768,512]{2,1,0:T(8,128)(2,1)S(1)} copy-done((bf16[8,768,512]{2,1,0:T(8,128)(2,1)S(1)}, bf16[8,768,512]{2,1,0:T(8,128)(2,1)}, u32[]{:S(2)}) %copy-start.2) | copy-done | bytes 6291480
  95.4 0.0 copy-start.3
  95.4 0.9 copy-done.3
  96.4 0.0 copy-start.4
  96.4 0.9 copy-done.4
  97.3 7.4 %shard_map.38 = f32[6144,256]{1,0:T(8,128)} custom-call(f32[6144,256]{1,0:T(8,128)S(1)} %copy-done, bf16[8,768,512]{2,1,0:T(8,128)(2,1)S(1)} %copy-done.1, bf16[8,768,512]{2,1,0:T(8,128)(2,1)S(1)} %copy-done.2, bf16[512,256]{1,0:T(8,128)(2,1)S(1)} %copy-done.3, bf16[512,256]{1,0:T(8,128)(2,1)S(1)} %copy-done.4), custom_call_target="tpu_custom_call" | custom-call | tf_op jit(solution)/shard_map/pallas_call | solution.py:351
Async XLA Ops:
  0.0 89.9 %copy-start = (f32[6144,256]{1,0:T(8,128)S(1)}, f32[6144,256]{1,0:T(8,128)}, u32[]{:S(2)}) copy-start(f32[6144,256]{1,0:T(8,128)} %x_ref.1) | copy-start | bytes 18874372
  89.9 2.8 %copy-start.1 = (bf16[8,768,512]{2,1,0:T(8,128)(2,1)S(1)}, bf16[8,768,512]{2,1,0:T(8,128)(2,1)}, u32[]{:S(2)}) copy-start(bf16[8,768,512]{2,1,0:T(8,128)(2,1)} %get-tuple-element.9.vh_ref) | copy-start | bytes 18874372
  92.6 2.8 %copy-start.2 = (bf16[8,768,512]{2,1,0:T(8,128)(2,1)S(1)}, bf16[8,768,512]{2,1,0:T(8,128)(2,1)}, u32[]{:S(2)}) copy-start(bf16[8,768,512]{2,1,0:T(8,128)(2,1)} %get-tuple-element.10.vl_ref) | copy-start | bytes 18874372
  95.4 0.9 copy-start.3
  96.4 0.9 copy-start.4

commit v3 on v2

--- a/solution.py
+++ b/solution.py
@@ -30,10 +30,10 @@
 NT = (((1,), (1,)), ((), ()))
 
 
-def gather_kernel(rows, vt_in, x_in, t_ref, wh_ref, wl_ref, vnh_out, vnl_out,
-                  vt, xb, xh, xl, vnh, vnl, pacc, pred, gacc, gh, gf, mref,
+def gather_kernel(rows, vt_in, x_in, t_ref, wh_ref, wl_ref, vnh, vnl, xb,
+                  vt, xh, xl, pacc, pred, gacc, gh, gf, mref,
                   rs_e, rs_g, rs_l,
-                  lsem, xsem, sbs, sbr, zs, zr, rss, rsr, ags, agr, gxs, gxr, osem):
+                  lsem, xsem, sbs, sbr, zs, zr, rss, rsr, ags, agr, gxs, gxr):
     me = lax.axis_index("row")
     col = lax.axis_index("col")
     z, k = lax.div(col, 2), lax.rem(col, 2)
@@ -125,10 +125,6 @@
             half = pl.ds(48, 32)
         return remote(gh.at[k, half], gh.at[k, half], gxs.at[i], gxr.at[i], (me, sib))
 
-    def store_out(c):
-        return (pltpu.make_async_copy(vnh.at[c], vnh_out.at[c], osem.at[0, c]),
-                pltpu.make_async_copy(vnl.at[c], vnl_out.at[c], osem.at[1, c]))
-
     def block(slot, c):
         return vt[slot, c].reshape(2 * vt.shape[3], lanes)
 
@@ -188,8 +184,10 @@
 
         @pl.when(c >= CHUNKS - 2)
         def _():
-            z_pass(0, c - (CHUNKS - 2)).start()
-            z_pass(1, c - (CHUNKS - 2)).start()
+            for i in range(2):
+                j = 2 * (c - (CHUNKS - 2)) + i
+                z_pass(0, j).start()
+                z_pass(1, j).start()
 
         to_sib(UP, c).start()
         to_sib(DOWN, c).start()
@@ -202,18 +200,12 @@
             c = j + i * (CHUNKS // 2)
             to_sib(FAR, c).wait_recv()
             apply(FAR, c, True)
-            a, b = store_out(c)
-            a.start()
-            b.start()
             return 0
         lax.fori_loop(0, 2, one, 0)
 
     def arrived(j):
         z_pass(0, j).wait_recv()
         z_pass(1, j).wait_recv()
-        if j + 2 < CHUNKS // 2:
-            z_pass(0, j + 2).start()
-            z_pass(1, j + 2).start()
         to_sib(FAR, j).start()
         to_sib(FAR, CHUNKS // 2 + j).start()
 
@@ -223,18 +215,20 @@
     arrived(0)
     sum_and_gather(1)
     far(0)
+    arrived(1)
     sum_and_gather(0)
     finish_gather(1)
-    gx(0).start()
-    gx(1).start()
-    gx(2).start()
-    arrived(1)
+    for i in range(3):
+        gx(i).start()
     far(1)
+    arrived(2)
     gx(0).wait_recv()
     gx(1).wait_recv()
     gx(3).start()
-    arrived(2)
     far(2)
+    arrived(3)
+    far(3)
+    reduce_scatter(2)
     gx(2).wait_recv()
     gx(3).wait_recv()
     for i, (r, s) in enumerate(GRAM):
@@ -252,12 +246,8 @@
             shard = lax.rem(z + REL[slot], 4)
             rest = unit - jnp.dot(gf[slot, slot, part, :], mref[slot], precision=HIGHEST)
             mref[slot, part, :] = jnp.dot(t_ref[4 * shard + i], rest, precision=HIGHEST)
+    sum_and_gather(2)
     finish_gather(0)
-
-    arrived(3)
-    far(3)
-    reduce_scatter(2)
-    sum_and_gather(2)
     finish_gather(2)
 
     def slot_of(shard):
@@ -280,8 +270,6 @@
             z_own(way, c).wait_send()
         for slot in range(4):
             to_sib(slot, c).wait_send()
-        for copy in store_out(c):
-            copy.wait()
         return 0
 
     lax.fori_loop(0, CHUNKS, sent, 0)
@@ -299,8 +287,20 @@
     each(sent_d)
 
 
-def update_kernel(x_ref, vh_ref, vl_ref, wh_ref, wl_ref, o_ref):
-    o_ref[...] = x_ref[...] - dot3((vh_ref[0], vl_ref[0]), (wh_ref[...], wl_ref[...]))
+def update_kernel(xb, vnh, vnl, wh_ref, wl_ref, out, buf, sem):
+    lanes = buf.shape[1]
+    w = wh_ref[...], wl_ref[...]
+
+    def store(c):
+        return pltpu.make_async_copy(buf.at[c], out.at[pl.ds(pl.multiple_of(c * lanes, lanes), lanes)], sem.at[c])
+
+    def one(c, _):
+        buf[c] = xb[c] - dot3((vnh[c], vnl[c]), w)
+        store(c).start()
+        return 0
+
+    lax.fori_loop(0, CHUNKS, one, 0)
+    lax.fori_loop(0, CHUNKS, lambda c, _: (store(c).wait(), 0)[1], 0)
 
 
 def on_device(rows, eigenvectors, reflectors, triangles):
@@ -310,23 +310,21 @@
     dma = pltpu.SemaphoreType.DMA
     anywhere = pl.BlockSpec(memory_space=pl.ANY)
     vmem = pl.BlockSpec(memory_space=pltpu.VMEM)
-    wh, wl, vnh, vnl = pl.pallas_call(
+    wh, wl, vnh, vnl, xb = pl.pallas_call(
         functools.partial(gather_kernel, rows),
         out_shape=[
-            jax.ShapeDtypeStruct((512, width), BF16),
-            jax.ShapeDtypeStruct((512, width), BF16),
-            jax.ShapeDtypeStruct((CHUNKS, lanes, 512), BF16),
-            jax.ShapeDtypeStruct((CHUNKS, lanes, 512), BF16),
+            pltpu.VMEM((512, width), BF16),
+            pltpu.VMEM((512, width), BF16),
+            pltpu.VMEM((CHUNKS, lanes, 512), BF16),
+            pltpu.VMEM((CHUNKS, lanes, 512), BF16),
+            pltpu.VMEM((CHUNKS, lanes, width), F32),
         ],
         in_specs=[anywhere, anywhere, vmem],
-        out_specs=[vmem, vmem, anywhere, anywhere],
+        out_specs=[vmem] * 5,
         scratch_shapes=[
             pltpu.VMEM((4, CHUNKS, 2, half, lanes), F32),
-            pltpu.VMEM((CHUNKS, lanes, width), F32),
             pltpu.VMEM((CHUNKS, lanes, width), BF16),
             pltpu.VMEM((CHUNKS, lanes, width), BF16),
-            pltpu.VMEM((CHUNKS, lanes, 512), BF16),
-            pltpu.VMEM((CHUNKS, lanes, 512), BF16),
             pltpu.VMEM((4, 16, 8, width), F32),
             pltpu.VMEM((4, 16, 8, width), F32),
             pltpu.VMEM((48, 8, 128), F32),
@@ -340,22 +338,19 @@
             dma((4, CHUNKS)), dma((4, CHUNKS)),
             dma((2, CHUNKS + CHUNKS // 2)), dma((2, CHUNKS + CHUNKS // 2)),
             dma((3, 16)), dma((3, 16)), dma((3, 16)), dma((3, 16)),
-            dma((4,)), dma((4,)), dma((2, CHUNKS)),
+            dma((4,)), dma((4,)),
         ],
         compiler_params=pltpu.CompilerParams(
-            collective_id=0, has_side_effects=True, vmem_limit_bytes=56 * 2**20),
+            collective_id=0, has_side_effects=True, vmem_limit_bytes=36 * 2**20),
     )(reflectors.T, eigenvectors, triangles)
-    whole = pl.BlockSpec((512, width), lambda i: (0, 0))
-    tall = pl.BlockSpec((1, lanes, 512), lambda i: (i, 0, 0))
-    rowwise = pl.BlockSpec((lanes, width), lambda i: (i, 0))
     return pl.pallas_call(
         update_kernel,
-        grid=(CHUNKS,),
         out_shape=jax.ShapeDtypeStruct((height, width), F32),
-        in_specs=[rowwise, tall, tall, whole, whole],
-        out_specs=rowwise,
-        compiler_params=pltpu.CompilerParams(vmem_limit_bytes=32 * 2**20),
-    )(eigenvectors, vnh, vnl, wh, wl)
+        in_specs=[vmem] * 5,
+        out_specs=anywhere,
+        scratch_shapes=[pltpu.VMEM((CHUNKS, lanes, width), F32), dma((CHUNKS,))],
+        compiler_params=pltpu.CompilerParams(vmem_limit_bytes=16 * 2**20),
+    )(xb, vnh, vnl, wh, wl)
 
 
 def solution(mesh):

time: 105 us -> 90.6 us (0.86)
  Pallas kernels: 97.3 us -> 89.8 us
  local copies, waits for them, and re-layouts: 7.46 us -> 0 us
    unnamed x10 -> x0, local copies, waits for them, and re-layouts: 7.46 us -> none
    pallas_call x2, Pallas kernels: 97.3 us -> 89.8 us  [the longest x1 82.5 us: on_device(): pl.pallas_call(functools.partial(gather_kernel, rows), out_shape=[pltpu.V...]
where the time goes in v3:
time: 90.6 us; the launch traced here: 89.8 us
  Pallas kernels  89.8 us (99%)
    pallas_call x1, Pallas kernels, on_device(): pl.pallas_call(functools.partial(gather_kernel, rows), out_shape=[pltpu.V...  82.5 us
    pallas_call x1, Pallas kernels, on_device(): pl.pallas_call(update_kernel, out_shape=jax.ShapeDtypeStruct((height, wid...  7.3 us

profile of v3, /device:TPU:0, one launch (start us, length us, event | category | flops | bytes accessed | tf_op | source)
XLA Modules:
  0.0 89.8 jit_solution(14891355131629404474)
XLA Ops:
  0.0 82.5 %shard_map.37 = (bf16[512,256]{1,0:T(8,128)(2,1)S(1)}, bf16[512,256]{1,0:T(8,128)(2,1)S(1)}, bf16[8,768,512]{2,1,0:T(8,128)(2,1)S(1)}, bf16[8,768,512]{2,1,0:T(8,128)(2,1)S(1)}, f32[8,768,256]{2,1,0:T(8,128)S(1)}) custom-call(f32[64,6144]{1,0:T(8,128)} %bitcast.1, f32[6144,256]{1,0:T(8,128)} %x_in.1, f32[16,32,32]{2,1,0:T(8,128)} %t_ref.1), custom_call_target="tpu_custom_call" | custom-call | tf_op jit(solution)/shard_map/pallas_call | solution.py:313
  82.5 7.3 %shard_map.38 = f32[6144,256]{1,0:T(8,128)} custom-call(f32[8,768,256]{2,1,0:T(8,128)S(1)} %get-tuple-element.10.xb, bf16[8,768,512]{2,1,0:T(8,128)(2,1)S(1)} %get-tuple-element.11.vnh, bf16[8,768,512]{2,1,0:T(8,128)(2,1)S(1)} %get-tuple-element.12.vnl, bf16[512,256]{1,0:T(8,128)(2,1)S(1)} %get-tuple-element.13.wh_ref, ...), custom_call_target="tpu_custom_call" | custom-call | tf_op jit(solution)/shard_map/pallas_call | solution.py:346

commit v4 on v3

v4 whole, which is shorter than its diff:
```python
import functools

import jax
import jax.numpy as jnp
from jax import lax
from jax.experimental import pallas as pl
from jax.experimental.pallas import tpu as pltpu
from jax.sharding import PartitionSpec as P

MESH = pl.DeviceIdType.MESH
F32, BF16 = jnp.float32, jnp.bfloat16
CHUNKS = 8
NEAR_SPLIT = 4
OWN, UP, DOWN, FAR = range(4)
REL = (0, 1, 3, 2)
GRAM = ((OWN, UP), (UP, UP), (OWN, DOWN), (UP, DOWN), (OWN, OWN), (DOWN, DOWN),
        (UP, FAR), (FAR, FAR), (DOWN, FAR), (OWN, FAR))


def split(a):
    high = a.astype(BF16)
    return high, (a - high.astype(F32)).astype(BF16)


def dot3(a, b, dims=(((1,), (0,)), ((), ()))):
    left = jnp.concatenate([a[0], a[0], a[1]], dims[0][0][0])
    right = jnp.concatenate([b[0], b[1], b[0]], dims[0][1][0])
    return lax.dot_general(left, right, dims, preferred_element_type=F32)


NT = (((1,), (1,)), ((), ()))


def dot(a, b):
    return dot3(split(a), split(b))


def gather_kernel(rows, vt_in, x_in, t_ref, rh_ref, rl_ref, vk, xb,
                  vt, xh, xl, vnh, vnl, wh, wl, wf, kh, kl, tb, pacc, pred, pred_l, gacc, gh, gf, mref,
                  rs_e, rs_g, rs_l,
                  xsem, own_in, near_in, far_in_sem, z_in, sib_out, z_out, rss, rsr, ags, agr, gxs, gxr, vks, vkr):
    me = lax.axis_index("row")
    col = lax.axis_index("col")
    z, k = lax.div(col, 2), lax.rem(col, 2)
    up = lax.rem(z + 1, 4) * 2 + k
    down = lax.rem(z + 3, 4) * 2 + k
    sib = z * 2 + 1 - k
    lanes = vt.shape[-1]

    barrier = pltpu.get_barrier_semaphore()
    for other in (up, down, sib):
        pl.semaphore_signal(barrier, inc=1, device_id=(me, other), device_id_type=MESH)
    for d in range(1, rows):
        pl.semaphore_signal(barrier, inc=1, device_id=(lax.rem(me + d, rows), col), device_id_type=MESH)

    def own(c):
        return vt_in.at[:, pl.ds(pl.multiple_of(c * lanes, lanes), lanes)]

    def local(c):
        return pltpu.make_async_copy(own(c), vt.at[OWN, c, k], own_in.at[c])

    def load_x(c):
        return pltpu.make_async_copy(x_in.at[pl.ds(pl.multiple_of(c * lanes, lanes), lanes)], xb.at[c], xsem.at[c])

    def remote(src, dst, ssem, rsem, target):
        return pltpu.make_async_remote_copy(src_ref=src, dst_ref=dst, send_sem=ssem, recv_sem=rsem,
                                            device_id=target, device_id_type=MESH)

    def z_own(way, c):
        return remote(own(c), vt.at[(UP, DOWN)[way], c, k], z_out, z_in.at[c], (me, (down, up)[way]))

    def z_pass(way, j):
        c = (j, CHUNKS // 2 + j)[way]
        return remote(vt.at[(UP, DOWN)[way], c, k], vt.at[FAR, c, k],
                      z_out, z_in.at[CHUNKS + j], (me, (down, up)[way]))

    def to_sib(slot, c):
        src = own(c) if slot == OWN else vt.at[slot, c, k]
        arrival = own_in.at[c] if slot == OWN else far_in_sem.at[lax.rem(c, CHUNKS // 2)] if slot == FAR else near_in.at[c]
        return remote(src, vt.at[slot, c, k], sib_out, arrival, (me, sib))

    def all_of(ref, sem):
        pltpu.make_async_copy(ref, ref, sem).wait()

    def peer(d):
        return lax.rem(me + d, rows)

    def rs(kind, d):
        p = peer(d)
        src = (pacc.at[pl.ds(0, 3), p], gacc.at[pl.ds(3 * p, 3)], pacc.at[pl.ds(3, 1), p])[kind]
        dst = (rs_e, rs_g, rs_l)[kind].at[d]
        return remote(src, dst, rss.at[kind], rsr.at[kind], (p, col))

    def piece(kind, owner):
        return (pred.at[pl.ds(0, 3), owner], gh.at[k, pl.ds(3 * owner, 3)], pred_l.at[pl.ds(0, 1), owner])[kind]

    def ag_send(kind, d):
        return remote(piece(kind, me), piece(kind, me), ags.at[kind], agr.at[kind], (peer(d), col))

    def others(kind):
        n = rows - 1
        return (rs_e.at[pl.ds(1, n)], rs_g.at[pl.ds(1, n)], rs_l.at[pl.ds(1, n)])[kind]

    def each(fn):
        lax.fori_loop(1, rows, lambda d, _: (fn(d), 0)[1], 0)

    def reduce_scatter(kind):
        each(lambda d: rs(kind, d).start())

    def sum_and_gather(kind):
        all_of(others(kind), rsr.at[kind])
        buf = (rs_e, rs_g, rs_l)[kind]
        total = (pacc[0:3, me], gacc[pl.ds(3 * me, 3)], pacc[3:4, me])[kind]
        for d in range(1, rows):
            total = total + buf[d]
        if kind == 1:
            gh[k, pl.ds(3 * me, 3)] = total
        elif kind == 0:
            pred[0:3, me] = total
        else:
            pred_l[0:1, me] = total
        each(lambda d: ag_send(kind, d).start())

    def finish_gather(kind):
        all_of(others(kind), agr.at[kind])

    def gx(i):
        half = pl.ds(0, 48)
        if i == 0:
            return remote(gh.at[k, pl.ds(0, 16)], gh.at[k, pl.ds(48, 16)], gxs.at[0], gxr.at[0], (me, down))
        if i == 1:
            return remote(gh.at[k, pl.ds(16, 16)], gh.at[k, pl.ds(64, 16)], gxs.at[1], gxr.at[1], (me, up))
        if i == 3:
            half = pl.ds(48, 32)
        return remote(gh.at[k, half], gh.at[k, half], gxs.at[i], gxr.at[i], (me, sib))

    def block(slot, c):
        return vt[slot, c].reshape(2 * vt.shape[3], lanes)

    def multiply(slot, c):
        pacc[slot] += dot3(split(block(slot, c)), (xh[c], xl[c])).reshape(16, 8, 256)

    def upright(slot, c):
        th, tl = split(block(slot, c).T)
        vnh[c, :, slot * 128:(slot + 1) * 128] = th
        vnl[c, :, slot * 128:(slot + 1) * 128] = tl

    def apply(slot, c):
        multiply(slot, c)
        upright(slot, c)

    def gram(c):
        v = [split(block(s, c)) for s in (OWN, UP, DOWN)]
        a = [split(vt[s, c, k]) for s in (OWN, UP, DOWN)]
        for i, (r, s) in enumerate(GRAM[:6]):
            gacc[8 * i:8 * i + 8] += dot3(a[r], v[s], NT).reshape(8, 8, 128)

    for c in range(CHUNKS):
        local(c).start()
        load_x(c).start()
    pl.semaphore_wait(barrier, rows + 2)
    for c in range(2):
        for way in range(2):
            z_own(way, c).start()
    for c in range(CHUNKS):
        to_sib(OWN, c).start()
    pacc[...] = jnp.zeros_like(pacc)
    gacc[...] = jnp.zeros_like(gacc)
    gf[...] = jnp.zeros_like(gf)
    mref[...] = jnp.zeros_like(mref)
    pred[3] = jnp.zeros_like(pred[3])
    tb[...] = jnp.zeros_like(tb)
    for slot in range(4):
        shard = lax.rem(z + REL[slot], 4)
        for i in range(4):
            tb[slot, 32 * i:32 * i + 32, 32 * i:32 * i + 32] = t_ref[4 * shard + i]

    def neighbours(c):
        all_of(vt.at[pl.ds(UP, 2), c, 1 - k], near_in.at[c])
        apply(UP, c)
        apply(DOWN, c)
        gram(c)

    def step(c, _):
        load_x(c).wait()
        h, l = split(xb[c])
        xh[c] = h
        xl[c] = l
        all_of(vt.at[OWN, c], own_in.at[c])
        apply(OWN, c)

        @pl.when(c > 0)
        def _():
            neighbours(c - 1)

        all_of(vt.at[pl.ds(UP, 2), c, k], z_in.at[c])

        @pl.when(c < CHUNKS - 2)
        def _():
            z_own(0, c + 2).start()
            z_own(1, c + 2).start()

        @pl.when(c >= CHUNKS - 2)
        def _():
            for i in range(2):
                j = 2 * (c - (CHUNKS - 2)) + i
                z_pass(0, j).start()
                z_pass(1, j).start()

        to_sib(UP, c).start()
        to_sib(DOWN, c).start()
        return 0

    lax.fori_loop(0, CHUNKS, step, 0)

    def far(j, *parts):
        def one(i, _):
            c = j + i * (CHUNKS // 2)
            for part in parts:
                part(c)
            return 0
        if far_in in parts:
            all_of(vt.at[FAR, pl.ds(0, 2), 1 - k], far_in_sem.at[j])
        lax.fori_loop(0, 2, one, 0)

    def far_in(c):
        multiply(FAR, c)

    def far_up(c):
        upright(FAR, c)

    def arrived(j):
        all_of(vt.at[FAR, pl.ds(0, 2), k], z_in.at[CHUNKS + j])
        to_sib(FAR, j).start()
        to_sib(FAR, CHUNKS // 2 + j).start()

    def slot_of(shard):
        rel = lax.rem(shard - z + 4, 4)
        return rel + lax.div(rel, 2) - 2 * lax.div(rel, 3)

    slots = [slot_of(s) for s in range(4)]

    def at_slot(s):
        return pl.ds(pl.multiple_of(slots[s] * 128, 128), 128)

    def assemble(first, last):
        for i in range(first, last):
            r, s = GRAM[i]
            full = gh[:, 8 * i:8 * i + 8].reshape(128, 128)
            gf[r, s] = full
            if r != s:
                gf[s, r] = full.T

    def invert(*which):
        row = lax.broadcasted_iota(jnp.int32, (128, 128), 0)
        lane = lax.broadcasted_iota(jnp.int32, (128, 128), 1)
        unit = jnp.where(lane == row, 1.0, 0.0).astype(F32)
        above = lane - lax.rem(lane, 32) > row
        n = [dot(tb[s], jnp.where(above, gf[s, s], 0.0)) for s in which]
        square = [dot(m, m) for m in n]
        both = [dot(unit - m, unit + q) for m, q in zip(n, square)]
        for s, m in zip(which, both):
            mref[s] = dot(m, tb[s])

    def substitute(rest, put):
        for s in range(3, -1, -1):
            w = dot(mref[slots[s]], rest[s])
            put(s, w)
            for r in range(s):
                rest[r] = rest[r] - dot(gf[slots[r], slots[s]], w)

    def near_w():
        def put(s, w):
            h, l = split(w)
            wh[at_slot(s)] = h
            wl[at_slot(s)] = l
            wf[slots[s]] = w
        substitute([pred[slots[s]].reshape(128, 256) for s in range(4)], put)

    def far_k():
        row = lax.broadcasted_iota(jnp.int32, (128, 128), 0)
        unit = jnp.where(lax.broadcasted_iota(jnp.int32, (128, 128), 1) == row, 1.0, 0.0).astype(F32)

        def put(s, w):
            h, l = split(w)
            kh[at_slot(s)] = h
            kl[at_slot(s)] = l
        substitute([jnp.where(slots[s] == FAR, unit, 0.0) for s in range(4)], put)

    def far_known():
        total = jnp.zeros((128, 256), F32)
        for slot in (OWN, UP, DOWN):
            after = lax.rem(z + REL[slot], 4) > lax.rem(z + 2, 4)
            total += jnp.where(after, dot(gf[FAR, slot], wf[slot]), 0.0)
        return total

    def near_update(first, last):
        def one(c, _):
            xb[c] -= dot3((vnh[c, :, :384], vnl[c, :, :384]), (wh[:384], wl[:384]))
            return 0
        lax.fori_loop(first, last, one, 0)

    def columns(c):
        return remote(vk.at[c], vk.at[c], vks, vkr, (me, sib))

    def far_columns():
        def one(i, _):
            c = k * (CHUNKS // 2) + i
            vk[c] = dot3((vnh[c], vnl[c]), (kh[...], kl[...]))
            columns(c).start()
            return 0
        lax.fori_loop(0, CHUNKS // 2, one, 0)

    neighbours(CHUNKS - 1)
    reduce_scatter(1)
    reduce_scatter(0)
    arrived(0)
    far(0, far_in, far_up)
    sum_and_gather(1)
    sum_and_gather(0)
    arrived(1)
    far(1, far_in, far_up)
    finish_gather(1)
    for i in range(3):
        gx(i).start()
    arrived(2)
    far(2, far_in, far_up)
    gx(2).wait_recv()
    assemble(0, 6)
    invert(OWN, UP, DOWN)
    finish_gather(0)
    arrived(3)
    near_w()
    far(3, far_in)
    reduce_scatter(2)
    gx(0).wait_recv()
    gx(1).wait_recv()
    gx(3).start()
    far(3, far_up)
    near_update(0, NEAR_SPLIT)
    gx(3).wait_recv()
    assemble(6, 10)
    invert(FAR)
    far_k()
    sum_and_gather(2)
    far_columns()
    known = far_known()
    near_update(NEAR_SPLIT, CHUNKS)
    finish_gather(2)
    h, l = split(pred_l[0].reshape(128, 256) - known)
    rh_ref[...] = h
    rl_ref[...] = l

    all_of(vk.at[pl.ds(0, CHUNKS // 2)], vkr)
    all_of(vk.at[pl.ds(0, CHUNKS // 2)], vks)
    all_of(vt.at[:, :, 0], sib_out)
    all_of(vt.at[pl.ds(0, 3), :, 0], z_out)
    for i in range(4):
        gx(i).wait_send()
    for kind in range(3):
        all_of(others(kind), rss.at[kind])
        all_of(others(kind), ags.at[kind])


def update_kernel(xb, vk, rh_ref, rl_ref, out, buf, sem):
    lanes = buf.shape[1]
    r = rh_ref[...], rl_ref[...]

    def store(c):
        return pltpu.make_async_copy(buf.at[c], out.at[pl.ds(pl.multiple_of(c * lanes, lanes), lanes)], sem.at[c])

    def one(c, _):
        change = dot3(split(vk[c]), r)
        buf[c] = xb[c] - jnp.where(change == change, change, 0.0)
        store(c).start()
        return 0

    lax.fori_loop(0, CHUNKS, one, 0)
    lax.fori_loop(0, CHUNKS, lambda c, _: (store(c).wait(), 0)[1], 0)


def on_device(rows, eigenvectors, reflectors, triangles):
    height, width = eigenvectors.shape
    lanes = height // CHUNKS
    half = reflectors.shape[1]
    dma = pltpu.SemaphoreType.DMA
    anywhere = pl.BlockSpec(memory_space=pl.ANY)
    vmem = pl.BlockSpec(memory_space=pltpu.VMEM)
    rh, rl, vk, xb = pl.pallas_call(
        functools.partial(gather_kernel, rows),
        out_shape=[
            pltpu.VMEM((128, width), BF16),
            pltpu.VMEM((128, width), BF16),
            pltpu.VMEM((CHUNKS, lanes, 128), F32),
            pltpu.VMEM((CHUNKS, lanes, width), F32),
        ],
        in_specs=[anywhere, anywhere, vmem],
        out_specs=[vmem] * 4,
        scratch_shapes=[
            pltpu.VMEM((4, CHUNKS, 2, half, lanes), F32),
            pltpu.VMEM((CHUNKS, lanes, width), BF16),
            pltpu.VMEM((CHUNKS, lanes, width), BF16),
            pltpu.VMEM((CHUNKS, lanes, 512), BF16),
            pltpu.VMEM((CHUNKS, lanes, 512), BF16),
            pltpu.VMEM((512, width), BF16),
            pltpu.VMEM((512, width), BF16),
            pltpu.VMEM((4, 128, width), F32),
            pltpu.VMEM((512, 128), BF16),
            pltpu.VMEM((512, 128), BF16),
            pltpu.VMEM((4, 128, 128), F32),
            pltpu.VMEM((4, 16, 8, width), F32),
            pltpu.VMEM((4, 16, 8, width), F32),
            pltpu.VMEM((1, 16, 8, width), F32),
            pltpu.VMEM((48, 8, 128), F32),
            pltpu.VMEM((2, 80, 8, 128), F32),
            pltpu.VMEM((4, 4, 128, 128), F32),
            pltpu.VMEM((4, 128, 128), F32),
            pltpu.VMEM((16, 3, 8, width), F32),
            pltpu.VMEM((16, 3, 8, 128), F32),
            pltpu.VMEM((16, 1, 8, width), F32),
            dma((CHUNKS,)), dma((CHUNKS,)), dma((CHUNKS,)), dma((CHUNKS // 2,)), dma((CHUNKS + CHUNKS // 2,)), dma, dma,
            dma((3,)), dma((3,)), dma((3,)), dma((3,)), dma((4,)), dma((4,)), dma, dma,
        ],
        compiler_params=pltpu.CompilerParams(
            collective_id=0, has_side_effects=True, vmem_limit_bytes=46 * 2**20),
    )(reflectors.T, eigenvectors, triangles)
    return pl.pallas_call(
        update_kernel,
        out_shape=jax.ShapeDtypeStruct((height, width), F32),
        in_specs=[vmem] * 4,
        out_specs=anywhere,
        scratch_shapes=[pltpu.VMEM((CHUNKS, lanes, width), F32), dma((CHUNKS,))],
        compiler_params=pltpu.CompilerParams(vmem_limit_bytes=16 * 2**20),
    )(xb, vk, rh, rl)


def solution(mesh):
    return jax.shard_map(
        functools.partial(on_device, mesh.shape["row"]),
        mesh=mesh,
        in_specs=(P("row", "col"), P("row", "col"), P()),
        out_specs=P("row", "col"),
        check_vma=False,
    )
```

time: 90.6 us -> 85.8 us (0.947)
  Pallas kernels: 89.8 us -> 85.2 us
    pallas_call x1, Pallas kernels: 7.3 us -> 3.9 us  [on_device(): pl.pallas_call(update_kernel, out_shape=jax.ShapeDtypeStruct((height, wid...]
    pallas_call x1, Pallas kernels: 82.5 us -> 81.3 us  [on_device(): pl.pallas_call(functools.partial(gather_kernel, rows), out_shape=[pltpu.V...]
where the time goes in v4:
time: 85.8 us; the launch traced here: 85.2 us
  Pallas kernels  85.2 us (99%)
    pallas_call x1, Pallas kernels, on_device(): pl.pallas_call(functools.partial(gather_kernel, rows), out_shape=[pltpu.V...  81.3 us
    pallas_call x1, Pallas kernels, on_device(): pl.pallas_call(update_kernel, out_shape=jax.ShapeDtypeStruct((height, wid...  3.9 us

profile of v4, /device:TPU:0, one launch (start us, length us, event | category | flops | bytes accessed | tf_op | source)
XLA Modules:
  0.0 85.2 jit_solution(7892894956577468991)
XLA Ops:
  0.0 81.3 %shard_map.37 = (bf16[128,256]{1,0:T(8,128)(2,1)S(1)}, bf16[128,256]{1,0:T(8,128)(2,1)S(1)}, f32[8,768,128]{2,1,0:T(8,128)S(1)}, f32[8,768,256]{2,1,0:T(8,128)S(1)}) custom-call(f32[64,6144]{1,0:T(8,128)} %bitcast.1, f32[6144,256]{1,0:T(8,128)} %x_in.1, f32[16,32,32]{2,1,0:T(8,128)} %t_ref.1), custom_call_target="tpu_custom_call" | custom-call | tf_op jit(solution)/shard_map/pallas_call | solution.py:389
  81.3 3.9 %shard_map.38 = f32[6144,256]{1,0:T(8,128)} custom-call(f32[8,768,256]{2,1,0:T(8,128)S(1)} %get-tuple-element.9.xb, f32[8,768,128]{2,1,0:T(8,128)S(1)} %get-tuple-element.10.vk, bf16[128,256]{1,0:T(8,128)(2,1)S(1)} %get-tuple-element.11.rh_ref, bf16[128,256]{1,0:T(8,128)(2,1)S(1)} %get-tuple-element.12.rl_ref), custom_call_target="tpu_custom_call" | custom-call | tf_op jit(solution)/shard_map/pallas_call | solution.py:427

commit v5 on v4

--- a/solution.py
+++ b/solution.py
@@ -10,7 +10,7 @@
 MESH = pl.DeviceIdType.MESH
 F32, BF16 = jnp.float32, jnp.bfloat16
 CHUNKS = 8
-NEAR_SPLIT = 4
+SIDE = 4
 OWN, UP, DOWN, FAR = range(4)
 REL = (0, 1, 3, 2)
 GRAM = ((OWN, UP), (UP, UP), (OWN, DOWN), (UP, DOWN), (OWN, OWN), (DOWN, DOWN),
@@ -35,10 +35,10 @@
     return dot3(split(a), split(b))
 
 
-def gather_kernel(rows, vt_in, x_in, t_ref, rh_ref, rl_ref, vk, xb,
-                  vt, xh, xl, vnh, vnl, wh, wl, wf, kh, kl, tb, pacc, pred, pred_l, gacc, gh, gf, mref,
-                  rs_e, rs_g, rs_l,
-                  xsem, own_in, near_in, far_in_sem, z_in, sib_out, z_out, rss, rsr, ags, agr, gxs, gxr, vks, vkr):
+def gather_kernel(rows, vt_in, x_in, t_ref, wh, wl, vnh, vnl, xb,
+                  vt, xh, xl, wf, kh, kl, tb, pacc, pred, pred_l, gacc, gh, gf, mref,
+                  rs_e, rs_g, rs_l, rs_o,
+                  xsem, own_in, near_in, far_in_sem, z_in, sib_out, z_out, rss, rsr, ags, agr, gxs, gxr, line_in):
     me = lax.axis_index("row")
     col = lax.axis_index("col")
     z, k = lax.div(col, 2), lax.rem(col, 2)
@@ -50,8 +50,10 @@
     barrier = pltpu.get_barrier_semaphore()
     for other in (up, down, sib):
         pl.semaphore_signal(barrier, inc=1, device_id=(me, other), device_id_type=MESH)
-    for d in range(1, rows):
-        pl.semaphore_signal(barrier, inc=1, device_id=(lax.rem(me + d, rows), col), device_id_type=MESH)
+    across = [lax.rem(me + SIDE * d, rows) for d in range(1, SIDE)]
+    along = [lax.div(me, SIDE) * SIDE + lax.rem(lax.rem(me, SIDE) + d, SIDE) for d in range(1, SIDE)]
+    for other in across + along:
+        pl.semaphore_signal(barrier, inc=1, device_id=(other, col), device_id_type=MESH)
 
     def own(c):
         return vt_in.at[:, pl.ds(pl.multiple_of(c * lanes, lanes), lanes)]
@@ -87,19 +89,20 @@
 
     def rs(kind, d):
         p = peer(d)
-        src = (pacc.at[pl.ds(0, 3), p], gacc.at[pl.ds(3 * p, 3)], pacc.at[pl.ds(3, 1), p])[kind]
-        dst = (rs_e, rs_g, rs_l)[kind].at[d]
+        src = (pacc.at[pl.ds(UP, 2), p], gacc.at[pl.ds(3 * p, 3)], pacc.at[pl.ds(FAR, 1), p], pacc.at[pl.ds(OWN, 1), p])[kind]
+        dst = (rs_e, rs_g, rs_l, rs_o)[kind].at[d]
         return remote(src, dst, rss.at[kind], rsr.at[kind], (p, col))
 
     def piece(kind, owner):
-        return (pred.at[pl.ds(0, 3), owner], gh.at[k, pl.ds(3 * owner, 3)], pred_l.at[pl.ds(0, 1), owner])[kind]
+        return (pred.at[pl.ds(UP, 2), owner], gh.at[k, pl.ds(3 * owner, 3)], pred_l.at[pl.ds(0, 1), owner],
+                pred.at[pl.ds(OWN, 1), owner])[kind]
 
     def ag_send(kind, d):
         return remote(piece(kind, me), piece(kind, me), ags.at[kind], agr.at[kind], (peer(d), col))
 
     def others(kind):
         n = rows - 1
-        return (rs_e.at[pl.ds(1, n)], rs_g.at[pl.ds(1, n)], rs_l.at[pl.ds(1, n)])[kind]
+        return (rs_e, rs_g, rs_l, rs_o)[kind].at[pl.ds(1, n)]
 
     def each(fn):
         lax.fori_loop(1, rows, lambda d, _: (fn(d), 0)[1], 0)
@@ -109,16 +112,18 @@
 
     def sum_and_gather(kind):
         all_of(others(kind), rsr.at[kind])
-        buf = (rs_e, rs_g, rs_l)[kind]
-        total = (pacc[0:3, me], gacc[pl.ds(3 * me, 3)], pacc[3:4, me])[kind]
+        buf = (rs_e, rs_g, rs_l, rs_o)[kind]
+        total = (pacc[UP:UP + 2, me], gacc[pl.ds(3 * me, 3)], pacc[FAR:FAR + 1, me], pacc[OWN:OWN + 1, me])[kind]
         for d in range(1, rows):
             total = total + buf[d]
         if kind == 1:
             gh[k, pl.ds(3 * me, 3)] = total
         elif kind == 0:
-            pred[0:3, me] = total
+            pred[UP:UP + 2, me] = total
+        elif kind == 2:
+            pred_l[0:1, me] = total
         else:
-            pred_l[0:1, me] = total
+            pred[OWN:OWN + 1, me] = total
         each(lambda d: ag_send(kind, d).start())
 
     def finish_gather(kind):
@@ -158,12 +163,14 @@
     for c in range(CHUNKS):
         local(c).start()
         load_x(c).start()
-    pl.semaphore_wait(barrier, rows + 2)
+    pl.semaphore_wait(barrier, 2 * SIDE + 1)
     for c in range(2):
         for way in range(2):
             z_own(way, c).start()
     for c in range(CHUNKS):
         to_sib(OWN, c).start()
+    for other in across:
+        pl.semaphore_signal(line_in, inc=1, device_id=(other, col), device_id_type=MESH)
     pacc[...] = jnp.zeros_like(pacc)
     gacc[...] = jnp.zeros_like(gacc)
     gf[...] = jnp.zeros_like(gf)
@@ -181,13 +188,28 @@
         apply(DOWN, c)
         gram(c)
 
-    def step(c, _):
+    def mine(c, _):
         load_x(c).wait()
         h, l = split(xb[c])
         xh[c] = h
         xl[c] = l
         all_of(vt.at[OWN, c], own_in.at[c])
         apply(OWN, c)
+        return 0
+
+    def step(c, _):
+        @pl.when(c < CHUNKS // 2)
+        def _():
+            lax.fori_loop(2 * c, 2 * c + 2, mine, 0)
+
+        @pl.when(c == CHUNKS // 2)
+        def _():
+            pl.semaphore_wait(line_in, SIDE - 1)
+            reduce_scatter(3)
+
+        @pl.when(c == CHUNKS - 2)
+        def _():
+            sum_and_gather(3)
 
         @pl.when(c > 0)
         def _():
@@ -271,9 +293,6 @@
 
     def near_w():
         def put(s, w):
-            h, l = split(w)
-            wh[at_slot(s)] = h
-            wl[at_slot(s)] = l
             wf[slots[s]] = w
         substitute([pred[slots[s]].reshape(128, 256) for s in range(4)], put)
 
@@ -294,88 +313,66 @@
             total += jnp.where(after, dot(gf[FAR, slot], wf[slot]), 0.0)
         return total
 
-    def near_update(first, last):
-        def one(c, _):
-            xb[c] -= dot3((vnh[c, :, :384], vnl[c, :, :384]), (wh[:384], wl[:384]))
-            return 0
-        lax.fori_loop(first, last, one, 0)
-
-    def columns(c):
-        return remote(vk.at[c], vk.at[c], vks, vkr, (me, sib))
-
-    def far_columns():
-        def one(i, _):
-            c = k * (CHUNKS // 2) + i
-            vk[c] = dot3((vnh[c], vnl[c]), (kh[...], kl[...]))
-            columns(c).start()
-            return 0
-        lax.fori_loop(0, CHUNKS // 2, one, 0)
-
     neighbours(CHUNKS - 1)
     reduce_scatter(1)
     reduce_scatter(0)
     arrived(0)
     far(0, far_in, far_up)
     sum_and_gather(1)
-    sum_and_gather(0)
     arrived(1)
     far(1, far_in, far_up)
+    sum_and_gather(0)
+    arrived(2)
+    far(2, far_in, far_up)
     finish_gather(1)
     for i in range(3):
         gx(i).start()
-    arrived(2)
-    far(2, far_in, far_up)
+    arrived(3)
+    far(3, far_in)
+    reduce_scatter(2)
+    far(3, far_up)
     gx(2).wait_recv()
     assemble(0, 6)
     invert(OWN, UP, DOWN)
-    finish_gather(0)
-    arrived(3)
-    near_w()
-    far(3, far_in)
-    reduce_scatter(2)
     gx(0).wait_recv()
     gx(1).wait_recv()
     gx(3).start()
-    far(3, far_up)
-    near_update(0, NEAR_SPLIT)
+    sum_and_gather(2)
+    finish_gather(3)
+    finish_gather(0)
+    near_w()
     gx(3).wait_recv()
     assemble(6, 10)
     invert(FAR)
     far_k()
-    sum_and_gather(2)
-    far_columns()
     known = far_known()
-    near_update(NEAR_SPLIT, CHUNKS)
     finish_gather(2)
-    h, l = split(pred_l[0].reshape(128, 256) - known)
-    rh_ref[...] = h
-    rl_ref[...] = l
-
-    all_of(vk.at[pl.ds(0, CHUNKS // 2)], vkr)
-    all_of(vk.at[pl.ds(0, CHUNKS // 2)], vks)
+    change = dot3((kh[...], kl[...]), split(pred_l[0].reshape(128, 256) - known))
+    h, l = split(wf[...].reshape(512, 256) + jnp.where(change == change, change, 0.0))
+    wh[...] = h
+    wl[...] = l
+
     all_of(vt.at[:, :, 0], sib_out)
     all_of(vt.at[pl.ds(0, 3), :, 0], z_out)
     for i in range(4):
         gx(i).wait_send()
-    for kind in range(3):
+    for kind in range(4):
         all_of(others(kind), rss.at[kind])
         all_of(others(kind), ags.at[kind])
 
 
-def update_kernel(xb, vk, rh_ref, rl_ref, out, buf, sem):
+def update_kernel(xb, vnh, vnl, wh, wl, out, buf, sem):
     lanes = buf.shape[1]
-    r = rh_ref[...], rl_ref[...]
 
     def store(c):
         return pltpu.make_async_copy(buf.at[c], out.at[pl.ds(pl.multiple_of(c * lanes, lanes), lanes)], sem.at[c])
 
     def one(c, _):
-        change = dot3(split(vk[c]), r)
-        buf[c] = xb[c] - jnp.where(change == change, change, 0.0)
+        buf[c] = xb[c] - dot3((vnh[c], vnl[c]), (wh[...], wl[...]))
         store(c).start()
         return 0
 
-    lax.fori_loop(0, CHUNKS, one, 0)
+    lax.fori_loop(0, CHUNKS, one, 0, unroll=2)
     lax.fori_loop(0, CHUNKS, lambda c, _: (store(c).wait(), 0)[1], 0)
 
 
@@ -386,24 +383,21 @@
     dma = pltpu.SemaphoreType.DMA
     anywhere = pl.BlockSpec(memory_space=pl.ANY)
     vmem = pl.BlockSpec(memory_space=pltpu.VMEM)
-    rh, rl, vk, xb = pl.pallas_call(
+    wh, wl, vnh, vnl, xb = pl.pallas_call(
         functools.partial(gather_kernel, rows),
         out_shape=[
-            pltpu.VMEM((128, width), BF16),
-            pltpu.VMEM((128, width), BF16),
-            pltpu.VMEM((CHUNKS, lanes, 128), F32),
+            pltpu.VMEM((512, width), BF16),
+            pltpu.VMEM((512, width), BF16),
+            pltpu.VMEM((CHUNKS, lanes, 512), BF16),
+            pltpu.VMEM((CHUNKS, lanes, 512), BF16),
             pltpu.VMEM((CHUNKS, lanes, width), F32),
         ],
         in_specs=[anywhere, anywhere, vmem],
-        out_specs=[vmem] * 4,
+        out_specs=[vmem] * 5,
         scratch_shapes=[
             pltpu.VMEM((4, CHUNKS, 2, half, lanes), F32),
             pltpu.VMEM((CHUNKS, lanes, width), BF16),
             pltpu.VMEM((CHUNKS, lanes, width), BF16),
-            pltpu.VMEM((CHUNKS, lanes, 512), BF16),
-            pltpu.VMEM((CHUNKS, lanes, 512), BF16),
-            pltpu.VMEM((512, width), BF16),
-            pltpu.VMEM((512, width), BF16),
             pltpu.VMEM((4, 128, width), F32),
             pltpu.VMEM((512, 128), BF16),
             pltpu.VMEM((512, 128), BF16),
@@ -415,23 +409,24 @@
             pltpu.VMEM((2, 80, 8, 128), F32),
             pltpu.VMEM((4, 4, 128, 128), F32),
             pltpu.VMEM((4, 128, 128), F32),
-            pltpu.VMEM((16, 3, 8, width), F32),
+            pltpu.VMEM((16, 2, 8, width), F32),
             pltpu.VMEM((16, 3, 8, 128), F32),
             pltpu.VMEM((16, 1, 8, width), F32),
+            pltpu.VMEM((16, 1, 8, width), F32),
             dma((CHUNKS,)), dma((CHUNKS,)), dma((CHUNKS,)), dma((CHUNKS // 2,)), dma((CHUNKS + CHUNKS // 2,)), dma, dma,
-            dma((3,)), dma((3,)), dma((3,)), dma((3,)), dma((4,)), dma((4,)), dma, dma,
+            dma((4,)), dma((4,)), dma((4,)), dma((4,)), dma((4,)), dma((4,)), pltpu.SemaphoreType.REGULAR,
         ],
         compiler_params=pltpu.CompilerParams(
-            collective_id=0, has_side_effects=True, vmem_limit_bytes=46 * 2**20),
+            collective_id=0, has_side_effects=True, vmem_limit_bytes=36 * 2**20),
     )(reflectors.T, eigenvectors, triangles)
     return pl.pallas_call(
         update_kernel,
         out_shape=jax.ShapeDtypeStruct((height, width), F32),
-        in_specs=[vmem] * 4,
+        in_specs=[vmem] * 5,
         out_specs=anywhere,
         scratch_shapes=[pltpu.VMEM((CHUNKS, lanes, width), F32), dma((CHUNKS,))],
         compiler_params=pltpu.CompilerParams(vmem_limit_bytes=16 * 2**20),
-    )(xb, vk, rh, rl)
+    )(xb, vnh, vnl, wh, wl)
 
 
 def solution(mesh):

time: 85.8 us -> 80.6 us (0.939)
  Pallas kernels: 85.2 us -> 80.4 us
    pallas_call x1, Pallas kernels: 81.3 us -> 73.4 us  [on_device(): pl.pallas_call(functools.partial(gather_kernel, rows), out_shape=[pltpu.V...]
    pallas_call x1, Pallas kernels: 3.9 us -> 6.96 us  [on_device(): pl.pallas_call(update_kernel, out_shape=jax.ShapeDtypeStruct((height, wid...]
where the time goes in v5:
time: 80.6 us; the launch traced here: 80.4 us
  Pallas kernels  80.4 us (100%)
    pallas_call x1, Pallas kernels, on_device(): pl.pallas_call(functools.partial(gather_kernel, rows), out_shape=[pltpu.V...  73.4 us
    pallas_call x1, Pallas kernels, on_device(): pl.pallas_call(update_kernel, out_shape=jax.ShapeDtypeStruct((height, wid...  6.96 us

profile of v5, /device:TPU:0, one launch (start us, length us, event | category | flops | bytes accessed | tf_op | source)
XLA Modules:
  0.0 80.4 jit_solution(1561928223094594874)
XLA Ops:
  0.0 73.4 %shard_map.37 = (bf16[512,256]{1,0:T(8,128)(2,1)S(1)}, bf16[512,256]{1,0:T(8,128)(2,1)S(1)}, bf16[8,768,512]{2,1,0:T(8,128)(2,1)S(1)}, bf16[8,768,512]{2,1,0:T(8,128)(2,1)S(1)}, f32[8,768,256]{2,1,0:T(8,128)S(1)}) custom-call(f32[64,6144]{1,0:T(8,128)} %bitcast.1, f32[6144,256]{1,0:T(8,128)} %x_in.1, f32[16,32,32]{2,1,0:T(8,128)} %t_ref.1), custom_call_target="tpu_custom_call" | custom-call | tf_op jit(solution)/shard_map/pallas_call | solution.py:386
  73.4 7.0 %shard_map.38 = f32[6144,256]{1,0:T(8,128)} custom-call(f32[8,768,256]{2,1,0:T(8,128)S(1)} %get-tuple-element.10.xb, bf16[8,768,512]{2,1,0:T(8,128)(2,1)S(1)} %get-tuple-element.11.vnh, bf16[8,768,512]{2,1,0:T(8,128)(2,1)S(1)} %get-tuple-element.12.vnl, bf16[512,256]{1,0:T(8,128)(2,1)S(1)} %get-tuple-element.13.wh, bf16[512,256]{1,0:T(8,128)(2,1)S(1)} %get-tuple-element.14.wl), custom_call_target="tpu_custom_call" | custom-call | tf_op jit(solution)/shard_map/pallas_call | solution.py:422

commit v6 on v5

--- a/solution.py
+++ b/solution.py
@@ -324,12 +324,12 @@
     sum_and_gather(0)
     arrived(2)
     far(2, far_in, far_up)
+    arrived(3)
+    far(3, far_in)
+    reduce_scatter(2)
     finish_gather(1)
     for i in range(3):
         gx(i).start()
-    arrived(3)
-    far(3, far_in)
-    reduce_scatter(2)
     far(3, far_up)
     gx(2).wait_recv()
     assemble(0, 6)
@@ -368,11 +368,14 @@
         return pltpu.make_async_copy(buf.at[c], out.at[pl.ds(pl.multiple_of(c * lanes, lanes), lanes)], sem.at[c])
 
     def one(c, _):
-        buf[c] = xb[c] - dot3((vnh[c], vnl[c]), (wh[...], wl[...]))
-        store(c).start()
+        two = pl.ds(2 * c, 2)
+        left = vnh[two].reshape(2 * lanes, 512), vnl[two].reshape(2 * lanes, 512)
+        buf[two] = xb[two] - dot3(left, (wh[...], wl[...])).reshape(2, lanes, 256)
+        store(2 * c).start()
+        store(2 * c + 1).start()
         return 0
 
-    lax.fori_loop(0, CHUNKS, one, 0, unroll=2)
+    lax.fori_loop(0, CHUNKS // 2, one, 0)
     lax.fori_loop(0, CHUNKS, lambda c, _: (store(c).wait(), 0)[1], 0)
 
 

time: 80.6 us -> 80.2 us (level)
  no operation moved by 1% of the time
where the time goes in v6:
time: 80.2 us; the launch traced here: 79.9 us
  Pallas kernels  79.9 us (100%)
    pallas_call x1, Pallas kernels, on_device(): pl.pallas_call(functools.partial(gather_kernel, rows), out_shape=[pltpu.V...  73.1 us
    pallas_call x1, Pallas kernels, on_device(): pl.pallas_call(update_kernel, out_shape=jax.ShapeDtypeStruct((height, wid...  6.8 us

profile of v6, /device:TPU:0, one launch (start us, length us, event | category | flops | bytes accessed | tf_op | source)
XLA Modules:
  0.0 79.9 jit_solution(4868819264196828018)
XLA Ops:
  0.0 73.1 %shard_map.37 = (bf16[512,256]{1,0:T(8,128)(2,1)S(1)}, bf16[512,256]{1,0:T(8,128)(2,1)S(1)}, bf16[8,768,512]{2,1,0:T(8,128)(2,1)S(1)}, bf16[8,768,512]{2,1,0:T(8,128)(2,1)S(1)}, f32[8,768,256]{2,1,0:T(8,128)S(1)}) custom-call(f32[64,6144]{1,0:T(8,128)} %bitcast.1, f32[6144,256]{1,0:T(8,128)} %x_in.1, f32[16,32,32]{2,1,0:T(8,128)} %t_ref.1), custom_call_target="tpu_custom_call" | custom-call | tf_op jit(solution)/shard_map/pallas_call | solution.py:389
  73.1 6.8 %shard_map.38 = f32[6144,256]{1,0:T(8,128)} custom-call(f32[8,768,256]{2,1,0:T(8,128)S(1)} %get-tuple-element.10.xb, bf16[8,768,512]{2,1,0:T(8,128)(2,1)S(1)} %get-tuple-element.11.vnh, bf16[8,768,512]{2,1,0:T(8,128)(2,1)S(1)} %get-tuple-element.12.vnl, bf16[512,256]{1,0:T(8,128)(2,1)S(1)} %get-tuple-element.13.wh, bf16[512,256]{1,0:T(8,128)(2,1)S(1)} %get-tuple-element.14.wl), custom_call_target="tpu_custom_call" | custom-call | tf_op jit(solution)/shard_map/pallas_call | solution.py:425

commit v7 on v6

--- a/solution.py
+++ b/solution.py
@@ -104,11 +104,15 @@
         n = rows - 1
         return (rs_e, rs_g, rs_l, rs_o)[kind].at[pl.ds(1, n)]
 
+    def far_first(fn):
+        for d in sorted(range(1, rows), key=lambda d: -sum(min(i, SIDE - i) for i in divmod(d, SIDE))):
+            fn(d)
+
     def each(fn):
         lax.fori_loop(1, rows, lambda d, _: (fn(d), 0)[1], 0)
 
     def reduce_scatter(kind):
-        each(lambda d: rs(kind, d).start())
+        (far_first if kind == 2 else each)(lambda d: rs(kind, d).start())
 
     def sum_and_gather(kind):
         all_of(others(kind), rsr.at[kind])
@@ -124,7 +128,7 @@
             pred_l[0:1, me] = total
         else:
             pred[OWN:OWN + 1, me] = total
-        each(lambda d: ag_send(kind, d).start())
+        (far_first if kind == 2 else each)(lambda d: ag_send(kind, d).start())
 
     def finish_gather(kind):
         all_of(others(kind), agr.at[kind])

time: 80.2 us -> 79.7 us (level)
  no operation moved by 1% of the time
where the time goes in v7:
time: 79.7 us; the launch traced here: 79.2 us
  Pallas kernels  79.2 us (99%)
    pallas_call x1, Pallas kernels, on_device(): pl.pallas_call(functools.partial(gather_kernel, rows), out_shape=[pltpu.V...  72.4 us
    pallas_call x1, Pallas kernels, on_device(): pl.pallas_call(update_kernel, out_shape=jax.ShapeDtypeStruct((height, wid...  6.8 us

profile of v7, /device:TPU:0, one launch (start us, length us, event | category | flops | bytes accessed | tf_op | source)
XLA Modules:
  0.0 79.2 jit_solution(10286057188268159821)
XLA Ops:
  0.0 72.4 %shard_map.37 = (bf16[512,256]{1,0:T(8,128)(2,1)S(1)}, bf16[512,256]{1,0:T(8,128)(2,1)S(1)}, bf16[8,768,512]{2,1,0:T(8,128)(2,1)S(1)}, bf16[8,768,512]{2,1,0:T(8,128)(2,1)S(1)}, f32[8,768,256]{2,1,0:T(8,128)S(1)}) custom-call(f32[64,6144]{1,0:T(8,128)} %bitcast.1, f32[6144,256]{1,0:T(8,128)} %x_in.1, f32[16,32,32]{2,1,0:T(8,128)} %t_ref.1), custom_call_target="tpu_custom_call" | custom-call | tf_op jit(solution)/shard_map/pallas_call | solution.py:393
  72.4 6.8 %shard_map.38 = f32[6144,256]{1,0:T(8,128)} custom-call(f32[8,768,256]{2,1,0:T(8,128)S(1)} %get-tuple-element.10.xb, bf16[8,768,512]{2,1,0:T(8,128)(2,1)S(1)} %get-tuple-element.11.vnh, bf16[8,768,512]{2,1,0:T(8,128)(2,1)S(1)} %get-tuple-element.12.vnl, bf16[512,256]{1,0:T(8,128)(2,1)S(1)} %get-tuple-element.13.wh, bf16[512,256]{1,0:T(8,128)(2,1)S(1)} %get-tuple-element.14.wl), custom_call_target="tpu_custom_call" | custom-call | tf_op jit(solution)/shard_map/pallas_call | solution.py:429
